TPU v7x, 256 devices: a whole 4x4x8 slice. The times are simulated.
256 devices in a mesh: ctx: 32 (over x_lo, z, core), head: 8 (over x_hi, y).
Axes of the slice: x: 4 (x_hi: 2, x_lo: 2; x = x_hi * 2 + x_lo), y: 4, z: 8, core: 2. Of those that a mesh axis runs over, the one named last changes fastest.
Arguments:
- asking_vectors: bfloat16 [65536, 32, 128], P('ctx', 'head'), as said below
- lookup_vectors: bfloat16 [65536, 32, 128], P('ctx', 'head'), as said below
- content_vectors: bfloat16 [65536, 32, 128], P('ctx', 'head'), may hold values from -6 to 6
- softmax_heat: float32 [32], P('head'), may hold values from 0.02 to 0.2
- document_places: int32 [65536], P('ctx'), may hold values from 0 to 4095, as said below
- digest_shifts: int32 [256, 8], P('ctx'), may hold values from 0 to 255, as said below
Outputs:
- attended: bfloat16 [65536, 32, 128], P(('ctx', 'head'))
Inputs may be any that keep to these rules, and one draw needn't show every extreme that they name: `digest_shifts`: the 8 offsets of one stride block are distinct. `document_places`: 0 at a document's first token (the sequence's first token is one) and one more than at the token before otherwise; no document is longer than min(4096, 16384) tokens, and the first one has exactly that length. `asking_vectors`: real-valued entries. `lookup_vectors`: real-valued entries.
All inputs are finite; a program needn't handle non-finite values.
Results may differ from a plain program's by a relative error of at most 0.006.
Values may be sent and summed in bfloat16 or wider, within the bound.
No kernel may reach another device: no remote copies, remote signals or barrier semaphores. Data moves between devices by JAX's collectives and lax.ppermute only.
A program may use at most 128 MiB of HBM per device.

v0:
```python
import math

import jax
import jax.numpy as jnp
from jax import lax
from jax.sharding import PartitionSpec as P


def band_scores(query_block, key_block, scale_block, stride_len):
    block_rows, heads_local, attender_dimension = query_block.shape
    groups = block_rows // stride_len
    query_groups = query_block.reshape(groups, stride_len, heads_local, attender_dimension)
    key_groups = key_block.reshape(groups, stride_len, heads_local, attender_dimension)
    raw_scores = jnp.einsum(
        "bqhd,bkhd->hbqk", query_groups, key_groups, preferred_element_type=jnp.float32
    )
    scale_groups = scale_block.T.reshape(heads_local, groups, stride_len, 1)
    inner_pos = jnp.arange(stride_len, dtype=jnp.int32)
    causal = inner_pos[:, None] >= inner_pos[None, :]
    return jnp.where(causal, raw_scores * scale_groups, -jnp.inf)


def band_values(band_prob, value_block, stride_len):
    block_rows, heads_local, attender_dimension = value_block.shape
    groups = block_rows // stride_len
    grouped_values = value_block.reshape(groups, stride_len, heads_local, attender_dimension)
    summed = jnp.einsum(
        "hbqk,bkhd->bqhd", band_prob, grouped_values, preferred_element_type=jnp.float32
    )
    return summed.reshape(block_rows, heads_local, attender_dimension)


def summary_scores(query_block, summary_keys, scale_block, summary_stride, query_stride):
    raw_scores = jnp.einsum(
        "qhd,shd->hqs", query_block, summary_keys, preferred_element_type=jnp.float32
    )
    seen_mask = summary_stride[None, :] < query_stride[:, None]
    return jnp.where(seen_mask[None], raw_scores * scale_block.T[:, :, None], -jnp.inf)


def direct_block(
    query_block,
    key_block,
    value_block,
    scale_block,
    query_stride,
    summary_keys,
    summary_values,
    summary_stride,
    stride_len,
):
    band = band_scores(query_block, key_block, scale_block, stride_len)
    summary = summary_scores(query_block, summary_keys, scale_block, summary_stride, query_stride)
    heads_local, groups = (band.shape[0], band.shape[1])
    top_score = jnp.maximum(band.max(-1).reshape(heads_local, -1), summary.max(-1))
    band_weight = jnp.exp(band - top_score.reshape(heads_local, groups, stride_len, 1))
    summary_column_weight = jnp.exp(summary - top_score[:, :, None])
    total_weight = band_weight.sum(-1).reshape(heads_local, -1) + summary_column_weight.sum(-1)
    numerator = band_values(band_weight.astype(jnp.bfloat16), value_block, stride_len)
    numerator = numerator + jnp.einsum(
        "hqs,shd->qhd",
        summary_column_weight.astype(jnp.bfloat16),
        summary_values,
        preferred_element_type=jnp.float32,
    )
    return (numerator / total_weight.T[:, :, None]).astype(jnp.bfloat16)


def per_device(
    asking_vectors, lookup_vectors, content_vectors, softmax_heat, document_places, digest_shifts
):
    tok_dev, heads_local, attender_dimension = asking_vectors.shape
    strides_local = digest_shifts.shape[0]
    summ_cols = digest_shifts.shape[1]
    stride_len = tok_dev // strides_local
    first_stride = lax.axis_index("ctx") * strides_local
    summary_rows = (
        jnp.arange(strides_local, dtype=jnp.int32)[:, None] * stride_len + digest_shifts
    ).reshape(-1)
    local_keys = jnp.take(lookup_vectors, summary_rows, axis=0)
    local_values = jnp.take(content_vectors, summary_rows, axis=0)
    log_of_place = jnp.log(1.0 + document_places.astype(jnp.float32))
    energy_multiplier = (1.0 + softmax_heat[None, :] * log_of_place[:, None]) / math.sqrt(
        attender_dimension
    )
    block_rows = min(tok_dev, 2 * stride_len)
    block_count = tok_dev // block_rows
    query_blocks = asking_vectors.reshape(block_count, block_rows, heads_local, attender_dimension)
    key_blocks = lookup_vectors.reshape(block_count, block_rows, heads_local, attender_dimension)
    value_blocks = content_vectors.reshape(block_count, block_rows, heads_local, attender_dimension)
    scale_blocks = energy_multiplier.reshape(block_count, block_rows, heads_local)
    query_strides = (first_stride + jnp.arange(tok_dev, dtype=jnp.int32) // stride_len).reshape(
        block_count, block_rows
    )
    summary_keys, summary_values = (
        lax.all_gather(local_keys, "ctx", axis=0, tiled=True),
        lax.all_gather(local_values, "ctx", axis=0, tiled=True),
    )
    summary_stride = jnp.arange(summary_keys.shape[0], dtype=jnp.int32) // summ_cols

    def one_direct(packed):
        return direct_block(
            packed[0],
            packed[1],
            packed[2],
            packed[3],
            packed[4],
            summary_keys,
            summary_values,
            summary_stride,
            stride_len,
        )

    attended = lax.map(
        one_direct, (query_blocks, key_blocks, value_blocks, scale_blocks, query_strides)
    )
    attended = attended.reshape(tok_dev, heads_local, attender_dimension)
    return lax.all_to_all(attended, "head", split_axis=0, concat_axis=1, tiled=True)


def solution(mesh):
    in_specs = (
        P("ctx", "head", None),
        P("ctx", "head", None),
        P("ctx", "head", None),
        P("head"),
        P("ctx"),
        P("ctx", None),
    )
    out_specs = P(("ctx", "head"), None, None)
    return jax.shard_map(
        per_device, mesh=mesh, in_specs=in_specs, out_specs=out_specs, check_vma=False
    )
```

profile of v0, /device:TPU:2, one launch (start us, length us, event | category | flops | bytes accessed | tf_op | source)
XLA Modules:
  0.0 316.9 jit_solution(17815822068971142666)
XLA Ops:
  6.5 0.8 broadcast_add_fusion
  7.4 2.2 gather_fusion
  9.7 2.2 gather_fusion.1
  11.9 0.8 broadcast_select_fusion
  12.8 0.7 all-gather.5.cloned.1.call-update
  13.5 0.7 add_log_fusion
  14.2 0.7 add_multiply_fusion
  15.0 65.1 %all-gather.3.cloned.1.call-done = bf16[2048,4,128]{2,1,0:T(4,128)(2,1)} async-done(((bf16[64,4,128]{2,1,0:T(4,128)(2,1)}), bf16[2048,4,128]{2,1,0:T(4,128)(2,1)}) %all-gather.3.cloned.1.call-update) | async-done | bytes 2097168 | tf_op jit(solution)/shard_map/all_gather | solution.py:96
  80.0 3.2 %copy.41 = bf16[2048,4,128]{2,0,1:T(8,128)(2,1)} copy(bf16[2048,4,128]{2,1,0:T(4,128)(2,1)} %all-gather.3.cloned.1.call-done) | data formatting | bytes 4194304
  83.2 63.1 %all-gather.5.cloned.1.call-done = bf16[2048,4,128]{2,1,0:T(4,128)(2,1)} async-done(((bf16[64,4,128]{2,1,0:T(4,128)(2,1)}), bf16[2048,4,128]{2,1,0:T(4,128)(2,1)}) %all-gather.5.cloned.1.call-update) | async-done | bytes 2097168 | tf_op jit(solution)/shard_map/all_gather | solution.py:97
  146.3 3.2 copy.42
  149.5 119.6 %while.11 = (s32[]{:T(128)}, bf16[4,512,4,128]{3,1,0,2:T(8,128)(2,1)}, bf16[4,512,4,128]{3,2,1,0:T(4,128)(2,1)}, bf16[4,512,4,128]{3,2,1,0:T(4,128)(2,1)}, bf16[...) while((s32[]{:T(128)}, ...), condition=%wide.region_5.7_spmd.clone, body=%wide.region_0.6_spmd.clone.sunk | while | flops 2468165632 | bytes 154098368 | solution.py:114
  149.5 1.6 constant_dynamic-slice_fusion.7
  151.3 0.5 fusion.60
  151.8 0.7 broadcast_compare_fusion.2
  152.4 0.4 copy-done.1
  152.8 3.9 %fusion.61 = (f32[4,512]{1,0:T(4,128)S(1)}, f32[4,512,2048]{2,1,0:T(8,128)S(1)}) fusion(f32[4,512]{1,0:T(4,128)S(1)} %dynamic-slice_bitcast_fusion.2, pred[512,2048]{1,0:T(8,128)(4,1)S(1)} %broadcast_compare_fusion.2, bf16[2048,4,128]{2,0,1:T(8,128)(2,1)S(1)} %copy-done.1, bf16[1,512,4,128]{3,2,1,0:T(4,128)(2,1)S(1)} %get-tuple-element.197), kind=kOutput, calls=%fused_computation.5.clone.1 | convolution fusion | flops 1086322688 | bytes 20463616 | tf_op jit(solution)/shard_map/while/body/eval_jaxpr/qhd,shd->hqs/dot_general | solution.py:34
  156.8 5.7 %copy-done = f32[4,512,2048]{2,1,0:T(8,128)} copy-done((f32[4,512,2048]{2,1,0:T(8,128)}, f32[4,512,2048]{2,1,0:T(8,128)S(1)}, u32[]{:S(2)}) %copy-start) | copy-done | bytes 16777240 | tf_op jit(solution)/shard_map/while
  162.5 4.6 %fusion.63 = f32[4,512]{1,0:T(4,128)S(1)} fusion(f32[4,512,2048]{2,1,0:T(8,128)S(1)} %get-tuple-element.203, f32[4,512]{1,0:T(4,128)S(1)} %max.18, f32[4,512]{1,0:T(4,128)S(1)} %dynamic-slice_bitcast_fusion.2, pred[512,2048]{1,0:T(8,128)(4,1)S(1)} %broadcast_compare_fusion.2), kind=kLoop, calls=%fused_computation.6.clone.1 | loop fusion | flops 16775168 | bytes 17850368 | tf_op jit(solution)/shard_map/while/body/eval_jaxpr/reduce_sum | solution.py:58
  167.2 0.5 fusion.62
  167.7 1.2 constant_dynamic-slice_fusion.9
  169.1 0.4 convolution_bitcast_fusion.2
  169.4 0.3 copy.90
  169.7 9.7 %fusion.64 = bf16[4,512,4,128]{3,1,0,2:T(8,128)(2,1)} fusion(bf16[4,512,4,128]{3,1,0,2:T(8,128)(2,1)} %get-tuple-element.216, s32[]{:T(128)} %get-tuple-element.215, f32[512,4,128]{2,0,1:T(8,128)S(1)} %bitcast.91, bf16[2048,4,128]{2,0,1:T(8,128)(2,1)} %get-tuple-element.233, f32[4,512,2048]{2,1,0:T(8,128)} %copy-done, f32[4,512]{1,0:T(4,128)S(1)} %max.18, ...), kind=kOutput, calls=%fused_computation.22.clone.1 | convolution fusion | flops 1091305472 | bytes 21520896 | tf_op jit(solution)/shard_map/while/body/eval_jaxpr/hqs,shd->qhd/dot_general | solution.py:60
  179.4 1.6 constant_dynamic-slice_fusion.7
  181.2 0.5 fusion.60
  181.7 0.7 broadcast_compare_fusion.2
  182.4 0.4 copy-done.1
  182.8 3.9 %fusion.61 = (f32[4,512]{1,0:T(4,128)S(1)}, f32[4,512,2048]{2,1,0:T(8,128)S(1)}) fusion(f32[4,512]{1,0:T(4,128)S(1)} %dynamic-slice_bitcast_fusion.2, pred[512,2048]{1,0:T(8,128)(4,1)S(1)} %broadcast_compare_fusion.2, bf16[2048,4,128]{2,0,1:T(8,128)(2,1)S(1)} %copy-done.1, bf16[1,512,4,128]{3,2,1,0:T(4,128)(2,1)S(1)} %get-tuple-element.197), kind=kOutput, calls=%fused_computation.5.clone.1 | convolution fusion | flops 1086322688 | bytes 20463616 | tf_op jit(solution)/shard_map/while/body/eval_jaxpr/qhd,shd->hqs/dot_general | solution.py:34
  186.7 5.7 %copy-done = f32[4,512,2048]{2,1,0:T(8,128)} copy-done((f32[4,512,2048]{2,1,0:T(8,128)}, f32[4,512,2048]{2,1,0:T(8,128)S(1)}, u32[]{:S(2)}) %copy-start) | copy-done | bytes 16777240 | tf_op jit(solution)/shard_map/while
  192.4 4.6 %fusion.63 = f32[4,512]{1,0:T(4,128)S(1)} fusion(f32[4,512,2048]{2,1,0:T(8,128)S(1)} %get-tuple-element.203, f32[4,512]{1,0:T(4,128)S(1)} %max.18, f32[4,512]{1,0:T(4,128)S(1)} %dynamic-slice_bitcast_fusion.2, pred[512,2048]{1,0:T(8,128)(4,1)S(1)} %broadcast_compare_fusion.2), kind=kLoop, calls=%fused_computation.6.clone.1 | loop fusion | flops 16775168 | bytes 17850368 | tf_op jit(solution)/shard_map/while/body/eval_jaxpr/reduce_sum | solution.py:58
  197.1 0.5 fusion.62
  197.6 1.2 constant_dynamic-slice_fusion.9
  199.0 0.4 convolution_bitcast_fusion.2
  199.3 0.3 copy.90
  199.7 9.7 %fusion.64 = bf16[4,512,4,128]{3,1,0,2:T(8,128)(2,1)} fusion(bf16[4,512,4,128]{3,1,0,2:T(8,128)(2,1)} %get-tuple-element.216, s32[]{:T(128)} %get-tuple-element.215, f32[512,4,128]{2,0,1:T(8,128)S(1)} %bitcast.91, bf16[2048,4,128]{2,0,1:T(8,128)(2,1)} %get-tuple-element.233, f32[4,512,2048]{2,1,0:T(8,128)} %copy-done, f32[4,512]{1,0:T(4,128)S(1)} %max.18, ...), kind=kOutput, calls=%fused_computation.22.clone.1 | convolution fusion | flops 1091305472 | bytes 21520896 | tf_op jit(solution)/shard_map/while/body/eval_jaxpr/hqs,shd->qhd/dot_general | solution.py:60
  209.3 1.6 constant_dynamic-slice_fusion.7
  211.1 0.5 fusion.60
  211.6 0.7 broadcast_compare_fusion.2
  212.3 0.4 copy-done.1
  212.7 3.9 %fusion.61 = (f32[4,512]{1,0:T(4,128)S(1)}, f32[4,512,2048]{2,1,0:T(8,128)S(1)}) fusion(f32[4,512]{1,0:T(4,128)S(1)} %dynamic-slice_bitcast_fusion.2, pred[512,2048]{1,0:T(8,128)(4,1)S(1)} %broadcast_compare_fusion.2, bf16[2048,4,128]{2,0,1:T(8,128)(2,1)S(1)} %copy-done.1, bf16[1,512,4,128]{3,2,1,0:T(4,128)(2,1)S(1)} %get-tuple-element.197), kind=kOutput, calls=%fused_computation.5.clone.1 | convolution fusion | flops 1086322688 | bytes 20463616 | tf_op jit(solution)/shard_map/while/body/eval_jaxpr/qhd,shd->hqs/dot_general | solution.py:34
  216.6 5.7 %copy-done = f32[4,512,2048]{2,1,0:T(8,128)} copy-done((f32[4,512,2048]{2,1,0:T(8,128)}, f32[4,512,2048]{2,1,0:T(8,128)S(1)}, u32[]{:S(2)}) %copy-start) | copy-done | bytes 16777240 | tf_op jit(solution)/shard_map/while
  222.3 4.6 %fusion.63 = f32[4,512]{1,0:T(4,128)S(1)} fusion(f32[4,512,2048]{2,1,0:T(8,128)S(1)} %get-tuple-element.203, f32[4,512]{1,0:T(4,128)S(1)} %max.18, f32[4,512]{1,0:T(4,128)S(1)} %dynamic-slice_bitcast_fusion.2, pred[512,2048]{1,0:T(8,128)(4,1)S(1)} %broadcast_compare_fusion.2), kind=kLoop, calls=%fused_computation.6.clone.1 | loop fusion | flops 16775168 | bytes 17850368 | tf_op jit(solution)/shard_map/while/body/eval_jaxpr/reduce_sum | solution.py:58
  227.0 0.5 fusion.62
  227.6 1.2 constant_dynamic-slice_fusion.9
  228.9 0.4 convolution_bitcast_fusion.2
  229.2 0.3 copy.90
  229.6 9.7 %fusion.64 = bf16[4,512,4,128]{3,1,0,2:T(8,128)(2,1)} fusion(bf16[4,512,4,128]{3,1,0,2:T(8,128)(2,1)} %get-tuple-element.216, s32[]{:T(128)} %get-tuple-element.215, f32[512,4,128]{2,0,1:T(8,128)S(1)} %bitcast.91, bf16[2048,4,128]{2,0,1:T(8,128)(2,1)} %get-tuple-element.233, f32[4,512,2048]{2,1,0:T(8,128)} %copy-done, f32[4,512]{1,0:T(4,128)S(1)} %max.18, ...), kind=kOutput, calls=%fused_computation.22.clone.1 | convolution fusion | flops 1091305472 | bytes 21520896 | tf_op jit(solution)/shard_map/while/body/eval_jaxpr/hqs,shd->qhd/dot_general | solution.py:60
  239.2 1.6 constant_dynamic-slice_fusion.7
  241.0 0.5 fusion.60
  241.5 0.7 broadcast_compare_fusion.2
  242.2 0.4 copy-done.1
  242.6 3.9 %fusion.61 = (f32[4,512]{1,0:T(4,128)S(1)}, f32[4,512,2048]{2,1,0:T(8,128)S(1)}) fusion(f32[4,512]{1,0:T(4,128)S(1)} %dynamic-slice_bitcast_fusion.2, pred[512,2048]{1,0:T(8,128)(4,1)S(1)} %broadcast_compare_fusion.2, bf16[2048,4,128]{2,0,1:T(8,128)(2,1)S(1)} %copy-done.1, bf16[1,512,4,128]{3,2,1,0:T(4,128)(2,1)S(1)} %get-tuple-element.197), kind=kOutput, calls=%fused_computation.5.clone.1 | convolution fusion | flops 1086322688 | bytes 20463616 | tf_op jit(solution)/shard_map/while/body/eval_jaxpr/qhd,shd->hqs/dot_general | solution.py:34
  246.5 5.7 %copy-done = f32[4,512,2048]{2,1,0:T(8,128)} copy-done((f32[4,512,2048]{2,1,0:T(8,128)}, f32[4,512,2048]{2,1,0:T(8,128)S(1)}, u32[]{:S(2)}) %copy-start) | copy-done | bytes 16777240 | tf_op jit(solution)/shard_map/while
  252.3 4.6 %fusion.63 = f32[4,512]{1,0:T(4,128)S(1)} fusion(f32[4,512,2048]{2,1,0:T(8,128)S(1)} %get-tuple-element.203, f32[4,512]{1,0:T(4,128)S(1)} %max.18, f32[4,512]{1,0:T(4,128)S(1)} %dynamic-slice_bitcast_fusion.2, pred[512,2048]{1,0:T(8,128)(4,1)S(1)} %broadcast_compare_fusion.2), kind=kLoop, calls=%fused_computation.6.clone.1 | loop fusion | flops 16775168 | bytes 17850368 | tf_op jit(solution)/shard_map/while/body/eval_jaxpr/reduce_sum | solution.py:58
  256.9 0.5 fusion.62
  257.5 1.2 constant_dynamic-slice_fusion.9
  258.8 0.4 convolution_bitcast_fusion.2
  259.1 0.3 copy.90
  259.5 9.7 %fusion.64 = bf16[4,512,4,128]{3,1,0,2:T(8,128)(2,1)} fusion(bf16[4,512,4,128]{3,1,0,2:T(8,128)(2,1)} %get-tuple-element.216, s32[]{:T(128)} %get-tuple-element.215, f32[512,4,128]{2,0,1:T(8,128)S(1)} %bitcast.91, bf16[2048,4,128]{2,0,1:T(8,128)(2,1)} %get-tuple-element.233, f32[4,512,2048]{2,1,0:T(8,128)} %copy-done, f32[4,512]{1,0:T(4,128)S(1)} %max.18, ...), kind=kOutput, calls=%fused_computation.22.clone.1 | convolution fusion | flops 1091305472 | bytes 21520896 | tf_op jit(solution)/shard_map/while/body/eval_jaxpr/hqs,shd->qhd/dot_general | solution.py:60
  269.1 3.4 %copy.44 = bf16[2048,4,128]{2,1,0:T(4,128)(2,1)S(1)} copy(bf16[2048,4,128]{2,0,1:T(8,128)(2,1)} %bitcast.95) | data formatting | bytes 4194304 | tf_op jit(solution)/shard_map/reshape | solution.py:117
  272.6 34.3 %all_to_all.18 = bf16[2048,4,128]{2,1,0:T(4,128)(2,1)S(1)} all-to-all(bf16[2048,4,128]{2,1,0:T(4,128)(2,1)S(1)} %copy.44), channel_id=1, replica_groups=mesh['ctx'=32,'head'=8] {'head'}, dimensions={0} | all-to-all | bytes 4194304 | tf_op jit(solution)/shard_map/all_to_all | solution.py:118
  306.9 0.3 copy.45
  307.4 2.7 copy.47
  (76 shorter events, 1.7 us)
Async XLA Ops:
  6.5 73.5 %all-gather.3.cloned.1.call-start = ((), (), s32[]{:S(2)}) async-start(), calls=%async_computation.1 | async-start | bytes 2162688 | tf_op jit(solution)/shard_map/all_gather | solution.py:96
  12.7 133.6 %all-gather.5.cloned.1.call-start = ((), (), s32[]{:S(2)}) async-start(), calls=%async_computation.2 | async-start | bytes 2162688 | tf_op jit(solution)/shard_map/all_gather | solution.py:97
  151.3 1.6 copy-start.1
  156.8 5.7 %copy-start = (f32[4,512,2048]{2,1,0:T(8,128)}, f32[4,512,2048]{2,1,0:T(8,128)S(1)}, u32[]{:S(2)}) copy-start(f32[4,512,2048]{2,1,0:T(8,128)S(1)} %get-tuple-element.203) | copy-start | bytes 50331652 | tf_op jit(solution)/shard_map/while
  181.2 1.6 copy-start.1
  186.7 5.7 %copy-start = (f32[4,512,2048]{2,1,0:T(8,128)}, f32[4,512,2048]{2,1,0:T(8,128)S(1)}, u32[]{:S(2)}) copy-start(f32[4,512,2048]{2,1,0:T(8,128)S(1)} %get-tuple-element.203) | copy-start | bytes 50331652 | tf_op jit(solution)/shard_map/while
  211.1 1.6 copy-start.1
  216.6 5.7 %copy-start = (f32[4,512,2048]{2,1,0:T(8,128)}, f32[4,512,2048]{2,1,0:T(8,128)S(1)}, u32[]{:S(2)}) copy-start(f32[4,512,2048]{2,1,0:T(8,128)S(1)} %get-tuple-element.203) | copy-start | bytes 50331652 | tf_op jit(solution)/shard_map/while
  241.0 1.6 copy-start.1
  246.5 5.7 %copy-start = (f32[4,512,2048]{2,1,0:T(8,128)}, f32[4,512,2048]{2,1,0:T(8,128)S(1)}, u32[]{:S(2)}) copy-start(f32[4,512,2048]{2,1,0:T(8,128)S(1)} %get-tuple-element.203) | copy-start | bytes 50331652 | tf_op jit(solution)/shard_map/while
Sparse Core Ops, SparseCore 0:
  12.8 67.1 all-gather.2
  81.9 64.3 all-gather.4
where the time goes:
time: 318 us; the launch traced here: 317 us
  waiting for transfers between devices  129 us (41%)
  matrix products  57.6 us (18%)
  local copies, waits for them, and re-layouts  55.6 us (17%)
  blocking collectives  34.3 us (11%)
  other arithmetic  26.5 us (8%)
  between operations  13.5 us (4%)
    all_gather x1, waiting for transfers between devices, per_device(): lax.all_gather(local_keys, 'ctx', axis=0, tiled=True)  65.1 us
    all_gather x1, waiting for transfers between devices, per_device(): lax.all_gather(local_values, 'ctx', axis=0, tiled=True)  63.1 us
    dot_general x4, matrix products, direct_block(): jnp.einsum('hqs,shd->qhd', summary_column_weight.astype(jnp.bfloat16), su...  38.6 us
    all_to_all x1, blocking collectives, per_device(): lax.all_to_all(attended, 'head', split_axis=0, concat_axis=1, tiled=True)  34.3 us
    while x24, local copies, waits for them, and re-layouts  24.5 us
    reduce_sum x4, other arithmetic, direct_block(): summary_column_weight.sum(-1)  18.6 us
    dot_general x4, matrix products, summary_scores(): jnp.einsum('qhd,shd->hqs', query_block, summary_keys, preferred_element_t...  15.7 us
    dynamic_slice x24, local copies, waits for them, and re-layouts, per_device(): lax.map(one_direct, (query_blocks, key_blocks, value_blocks, scale_blocks...  12 us
  transfers between devices with their start and end apart: 2, of which 2 were waited for; matrix products, arithmetic and copies ran while one was open for 1% of the time, Pallas kernels for 0%

commit v1 on v0

v1 whole, which is shorter than its diff:
```python
import functools
import math

import jax
import jax.numpy as jnp
from jax import lax
from jax.experimental import pallas as pl
from jax.experimental.pallas import tpu as pltpu
from jax.sharding import Mesh
from jax.sharding import PartitionSpec as P

F32, BF16 = jnp.float32, jnp.bfloat16
NEG = -1e30
STRIDE, SUMM, DIM, HEADS = 256, 8, 128, 4
BLOCKS = 8
COLS = BLOCKS * SUMM
CHIPS = 8
GROUP = 2
TRANS_B = (((1,), (1,)), ((), ()))
CTX = ("x_lo", "z", "core")
HEAD = ("x_hi", "y")


def gather_kernel(shift_ref, k_hbm, v_hbm, out0_ref, out1_ref, rows_ref, wide_ref, sems):
    for w, hbm in enumerate((k_hbm, v_hbm)):
        for c in range(COLS):
            row = (c // SUMM) * STRIDE + shift_ref[c // SUMM, c % SUMM]
            pltpu.make_async_copy(
                hbm.at[pl.ds(row, 1)], rows_ref.at[w, pl.ds(c, 1)], sems.at[w]
            ).start()
    for w, hbm in enumerate((k_hbm, v_hbm)):
        pltpu.make_async_copy(hbm.at[pl.ds(0, COLS)], rows_ref.at[w], sems.at[w]).wait()
        for c in range(COLS):
            wide_ref[w, pl.ds(c * HEADS, HEADS), :] = rows_ref[w, c].astype(F32)
        for h in range(HEADS):
            out_ref = (out0_ref, out1_ref)[h // GROUP]
            x = wide_ref[w, pl.ds(h, COLS, stride=HEADS), :].astype(BF16)
            for d in range(CHIPS):
                out_ref[d, w, h % GROUP] = x


def gather_summaries(digest_shifts, keys, values):
    out = jax.ShapeDtypeStruct((CHIPS, 2, GROUP, COLS, DIM), BF16)
    return pl.pallas_call(
        gather_kernel,
        in_specs=[
            pl.BlockSpec(memory_space=pltpu.SMEM),
            pl.BlockSpec(memory_space=pl.ANY),
            pl.BlockSpec(memory_space=pl.ANY),
        ],
        out_shape=[out, out],
        scratch_shapes=[
            pltpu.VMEM((2, COLS, HEADS, DIM), BF16),
            pltpu.VMEM((2, COLS * HEADS, DIM), F32),
            pltpu.SemaphoreType.DMA((2,)),
        ],
        name="gather_summaries",
    )(digest_shifts, keys, values)


def attend(q, keys, values, biases, m, l, acc):
    scores = []
    for k, bias in zip(keys, biases):
        s = lax.dot_general(
            q, jnp.concatenate([k, k], axis=1), TRANS_B, preferred_element_type=F32
        )
        scores.append(s if bias is None else s + bias)
    top = m
    for s in scores:
        peak = s.max(axis=1, keepdims=True)
        top = peak if top is None else jnp.maximum(top, peak)
    if m is not None:
        shrink = jnp.exp2(m - top)
        acc, l = acc * shrink, l * shrink
    for s, v in zip(scores, values):
        p = jnp.exp2(s - top).astype(BF16)
        o = jnp.dot(
            p, jnp.concatenate([v, jnp.ones_like(v)], axis=1), preferred_element_type=F32
        )
        acc = o[:, :DIM] if acc is None else acc + o[:, :DIM]
        l = o[:, DIM:] if l is None else l + o[:, DIM:]
    return top, l, acc


def pack_stats(m, l):
    lane = lax.broadcasted_iota(jnp.int32, l.shape, 1)
    return jnp.where(lane < DIM // 2, m, l)


def unpack_stats(ml):
    return ml[:, 0:1], jnp.broadcast_to(ml[:, DIM // 2 : DIM // 2 + 1], ml.shape)


def band_kernel(heat_ref, place_ref, q_ref, k_ref, v_ref, qs_ref, acc_ref, ml_ref, wide_ref):
    j = pl.program_id(0)
    place = place_ref[pl.ds(j, 1), :].astype(F32)
    log_place = jnp.broadcast_to(jnp.log(1.0 + place), (8, STRIDE))
    scale = (1.0 + heat_ref[...] * log_place) * (math.log2(math.e) / math.sqrt(DIM))
    scale = scale.T
    for w, ref in enumerate((q_ref, k_ref, v_ref)):
        wide_ref[w] = ref[...].astype(F32)
    inner = [lax.broadcasted_iota(jnp.int32, (STRIDE, STRIDE), d) for d in range(2)]
    bias = jnp.where(inner[0] >= inner[1], 0.0, NEG)
    for h in range(HEADS):
        q, k, v = (wide_ref[w, pl.ds(h, STRIDE, stride=HEADS), :] for w in range(3))
        q = q * scale[:, h : h + 1]
        high = q.astype(BF16)
        low = (q - high.astype(F32)).astype(BF16)
        q = jnp.concatenate([high, low], axis=1)
        m, l, acc = attend(q, (k.astype(BF16),), (v.astype(BF16),), (bias,), None, None, None)
        qs_ref[h] = q
        acc_ref[h] = acc
        ml_ref[h] = pack_stats(m, l)


def band(heat, places, q, k, v):
    tokens = BLOCKS * STRIDE
    whole = lambda *s: pl.BlockSpec(s, lambda j: (0,) * len(s))
    rows = pl.BlockSpec((STRIDE * HEADS, DIM), lambda j: (j, 0))
    out = lambda d: pl.BlockSpec((HEADS, STRIDE, d), lambda j: (0, j, 0))
    shape = lambda d, t: jax.ShapeDtypeStruct((HEADS, tokens, d), t)
    return pl.pallas_call(
        band_kernel,
        grid=(BLOCKS,),
        in_specs=[whole(8, 1), whole(BLOCKS, STRIDE), rows, rows, rows],
        out_specs=[out(2 * DIM), out(DIM), out(DIM)],
        out_shape=[shape(2 * DIM, BF16), shape(DIM, F32), shape(DIM, F32)],
        scratch_shapes=[pltpu.VMEM((3, STRIDE * HEADS, DIM), F32)],
        compiler_params=pltpu.CompilerParams(vmem_limit_bytes=32 << 20),
        cost_estimate=pl.CostEstimate(
            flops=4 * HEADS * tokens * STRIDE * DIM * 2, bytes_accessed=20 << 20,
            transcendentals=HEADS * tokens * STRIDE,
        ),
        name="band",
    )(heat, places, q, k, v)


def own_kernel(at_ref, q_ref, km_ref, ko_ref, vm_ref, vo_ref, acc_ref, ml_ref, acc_out, ml_out):
    z, core = at_ref[1], at_ref[2]
    flat = lambda ref: ref[...].reshape(CHIPS * COLS, DIM)
    keys, values = (flat(km_ref), flat(ko_ref)), (flat(vm_ref), flat(vo_ref))
    col = lax.broadcasted_iota(jnp.int32, (1, CHIPS * COLS), 1)
    other = jnp.where(col < (z + core) * COLS, 0.0, NEG)
    for j in range(BLOCKS):
        rows = pl.ds(j * STRIDE, STRIDE)
        mine = jnp.where(col < z * COLS + SUMM * j, 0.0, NEG)
        m, l = unpack_stats(ml_ref[0, rows, :])
        m, l, acc = attend(q_ref[0, rows, :], keys, values, (mine, other), m, l, acc_ref[0, rows, :])
        acc_out[0, rows, :] = acc
        ml_out[0, rows, :] = pack_stats(m, l)


def far_kernel(at_ref, q_ref, km_ref, ko_ref, vm_ref, vo_ref, acc_ref, ml_ref, out_ref):
    x = at_ref[0]

    @pl.when(x == 1)
    def _():
        flat = lambda ref: ref[...].reshape(CHIPS * COLS, DIM)
        keys, values = (flat(km_ref), flat(ko_ref)), (flat(vm_ref), flat(vo_ref))
        for j in range(BLOCKS):
            rows = pl.ds(j * STRIDE, STRIDE)
            m, l = unpack_stats(ml_ref[0, rows, :])
            m, l, acc = attend(
                q_ref[0, rows, :], keys, values, (None, None), m, l, acc_ref[0, rows, :]
            )
            out_ref[j, 0] = (acc / l).astype(BF16)

    @pl.when(x == 0)
    def _():
        for j in range(BLOCKS):
            rows = pl.ds(j * STRIDE, STRIDE)
            _, l = unpack_stats(ml_ref[0, rows, :])
            out_ref[j, 0] = (acc_ref[0, rows, :] / l).astype(BF16)


def summaries(kernel, at, q, mine, other, acc, ml, group, name, out_specs, out_shape):
    tokens = BLOCKS * STRIDE
    first = group * GROUP
    kv = lambda w: pl.BlockSpec((CHIPS, 1, 1, COLS, DIM), lambda h: (0, w, h, 0, 0))
    state = lambda d, at=0: pl.BlockSpec((1, tokens, d), lambda h: (h + at, 0, 0))
    shift = first if acc.shape[0] == HEADS else 0
    return pl.pallas_call(
        kernel,
        grid=(GROUP,),
        in_specs=[
            pl.BlockSpec(memory_space=pltpu.SMEM),
            state(2 * DIM, first),
            kv(0), kv(0), kv(1), kv(1),
            state(DIM, shift), state(DIM, shift),
        ],
        out_specs=out_specs,
        out_shape=out_shape,
        compiler_params=pltpu.CompilerParams(vmem_limit_bytes=48 << 20),
        cost_estimate=pl.CostEstimate(
            flops=4 * GROUP * tokens * 2 * CHIPS * COLS * DIM * 2, bytes_accessed=12 << 20,
            transcendentals=GROUP * tokens * 2 * CHIPS * COLS,
        ),
        name=name,
    )(at, q, mine, other, mine, other, acc, ml)


def own_summaries(at, q, mine, other, acc, ml, group):
    tokens = BLOCKS * STRIDE
    spec = pl.BlockSpec((1, tokens, DIM), lambda h: (h, 0, 0))
    shape = jax.ShapeDtypeStruct((GROUP, tokens, DIM), F32)
    return summaries(
        own_kernel, at, q, mine, other, acc, ml, group, f"own_{group}", [spec] * 2, [shape] * 2
    )


def far_summaries(at, q, mine, other, acc, ml, group):
    spec = pl.BlockSpec((BLOCKS, 1, STRIDE, DIM), lambda h: (0, h, 0, 0))
    shape = jax.ShapeDtypeStruct((BLOCKS, GROUP, STRIDE, DIM), BF16)
    return summaries(far_kernel, at, q, mine, other, acc, ml, group, f"far_{group}", spec, shape)


def assemble_kernel(x0_ref, x1_ref, out_ref, wide_ref):
    count = x0_ref.shape[2]
    total = BLOCKS * HEADS
    for source in range(BLOCKS):
        for h in range(HEADS):
            ref = (x0_ref, x1_ref)[h // GROUP]
            wide_ref[pl.ds(source * HEADS + h, count, stride=total), :] = ref[
                source, h % GROUP
            ].astype(F32)
    out_ref[...] = wide_ref[...].astype(BF16)


def assemble(x0, x1, steps=4):
    count = STRIDE // steps
    total = BLOCKS * HEADS
    spec = pl.BlockSpec((BLOCKS, GROUP, count, DIM), lambda t: (0, 0, t, 0))
    return pl.pallas_call(
        assemble_kernel,
        grid=(steps,),
        in_specs=[spec, spec],
        out_specs=pl.BlockSpec((count * total, DIM), lambda t: (t, 0)),
        out_shape=jax.ShapeDtypeStruct((STRIDE * total, DIM), BF16),
        scratch_shapes=[pltpu.VMEM((count * total, DIM), F32)],
        name="assemble",
    )(x0, x1)


def per_device(q, k, v, heat, places, shifts):
    at = jnp.stack([lax.axis_index(a) for a in CTX]).astype(jnp.int32)
    tokens = BLOCKS * STRIDE
    sends = gather_summaries(shifts, k, v)
    mine = [lax.all_to_all(s, "z", 0, 0, tiled=True) for s in sends]
    heat8 = jnp.pad(heat, (0, 8 - HEADS)).reshape(8, 1)
    flat = lambda x: x.reshape(tokens * HEADS, DIM)
    qs, acc, ml = band(heat8, places.reshape(BLOCKS, STRIDE), flat(q), flat(k), flat(v))
    swap = [(0, 1), (1, 0)]
    mine[0], mine[1], qs, acc, ml = lax.optimization_barrier((mine[0], mine[1], qs, acc, ml))
    parts = []
    for g in range(2):
        other = lax.ppermute(mine[g], "core", swap)
        far_mine = lax.ppermute(mine[g], "x_lo", [(0, 1)])
        far_other = lax.ppermute(far_mine, "core", swap)
        acc_g, ml_g = own_summaries(at, qs, mine[g], other, acc, ml, g)
        out = far_summaries(at, qs, far_mine, far_other, acc_g, ml_g, g)
        parts.append(lax.all_to_all(out, HEAD, 0, 0, tiled=True))
    return assemble(*parts).reshape(STRIDE, BLOCKS * HEADS, DIM)


def solution(mesh):
    devices = mesh.devices
    wide = Mesh(devices.reshape(2, 8, 2, 2, 4), CTX + HEAD)
    in_specs = (
        P(CTX, HEAD, None),
        P(CTX, HEAD, None),
        P(CTX, HEAD, None),
        P(HEAD),
        P(CTX),
        P(CTX, None),
    )
    return jax.shard_map(
        per_device, mesh=wide, in_specs=in_specs, out_specs=P(CTX + HEAD, None, None),
        check_vma=False,
    )
```

time: 318 us -> 151 us (0.47)
  waiting for transfers between devices: 129 us -> 21.7 us
  matrix products: 57.6 us -> 0 us
  Pallas kernels: 0 us -> 53.1 us
  local copies, waits for them, and re-layouts: 55.6 us -> 11.8 us
  other arithmetic: 26.5 us -> 0.08 us
  blocking collectives: 34.3 us -> 50.5 us
  between operations: 13.5 us -> 0.17 us
  starting transfers between devices: 0.04 us -> 12.7 us
    all_gather x2 -> x0, waiting for transfers between devices: 128 us -> none  [the longest x1 65.1 us: per_device(): lax.all_gather(local_keys, 'ctx', axis=0, tiled=True)]
    dot_general x16 -> x0, matrix products: 57.6 us -> none  [the longest x4 38.6 us: direct_block(): jnp.einsum('hqs,shd->qhd', summary_column_weight.astype(jnp.bfloat16), su...]
    pallas_call x0 -> x7, Pallas kernels: none -> 53.1 us  [the longest x4 33.6 us: summaries(): pl.pallas_call(kernel, grid=(GROUP,), in_specs=[pl.BlockSpec(memory_space...]
    while x24 -> x0, local copies, waits for them, and re-layouts: 24.5 us -> none
    ppermute x0 -> x6, waiting for transfers between devices: none -> 21.7 us  [the longest x2 21.7 us: per_device(): far_mine = lax.ppermute(mine[g], 'x_lo', [(0, 1)])]
    reduce_sum x8 -> x0, other arithmetic: 20.6 us -> none  [the longest x4 18.6 us: direct_block(): summary_column_weight.sum(-1)]
    all_to_all x1 -> x2, blocking collectives: 34.3 us -> 50.5 us  [the longest x1 26.1 us: per_device(): mine = [lax.all_to_all(s, 'z', 0, 0, tiled=True) for s in sends]]
    dynamic_slice x24 -> x0, local copies, waits for them, and re-layouts: 12 us -> none  [per_device(): lax.map(one_direct, (query_blocks, key_blocks, value_blocks, scale_blocks...]
  transfers between devices with their start and end apart: 2 -> 8, of which waited for: 2 -> 2; matrix products, arithmetic and copies ran while one was open for 1% -> 0% of each run, Pallas kernels for 0% -> 29%
where the time goes in v1:
time: 151 us; the launch traced here: 150 us
  Pallas kernels  53.1 us (35%)
  blocking collectives  50.5 us (33%)
  waiting for transfers between devices  21.7 us (14%)
  starting transfers between devices  12.7 us (8%)
  local copies, waits for them, and re-layouts  11.8 us (8%)
    pallas_call x4, Pallas kernels, summaries(): pl.pallas_call(kernel, grid=(GROUP,), in_specs=[pl.BlockSpec(memory_space...  33.6 us
    all_to_all x1, blocking collectives, per_device(): mine = [lax.all_to_all(s, 'z', 0, 0, tiled=True) for s in sends]  26.1 us
    all_to_all x1, blocking collectives, per_device(): parts.append(lax.all_to_all(out, HEAD, 0, 0, tiled=True))  24.4 us
    ppermute x2, waiting for transfers between devices, per_device(): far_mine = lax.ppermute(mine[g], 'x_lo', [(0, 1)])  21.7 us
    unnamed x20, local copies, waits for them, and re-layouts  11.7 us
    pallas_call x1, Pallas kernels, band(): pl.pallas_call(band_kernel, grid=(BLOCKS,), in_specs=[whole(8, 1), whole(...  9.9 us
    pallas_call x1, Pallas kernels, assemble(): pl.pallas_call(assemble_kernel, grid=(steps,), in_specs=[spec, spec], out...  6.36 us
    all_to_all x1, starting transfers between devices, per_device(): parts.append(lax.all_to_all(out, HEAD, 0, 0, tiled=True))  6.03 us
  transfers between devices with their start and end apart: 8, of which 2 were waited for; matrix products, arithmetic and copies ran while one was open for 0% of the time, Pallas kernels for 29%

profile of v1, /device:TPU:2, one launch (start us, length us, event | category | flops | bytes accessed | tf_op | source)
XLA Modules:
  0.0 150.1 jit_solution(4559903053257274577)
XLA Ops:
  0.0 0.0 copy-start.8
  0.0 3.2 %gather_summaries.1 = (bf16[8,2,2,64,128]{4,3,2,1,0:T(8,128)(2,1)}, bf16[8,2,2,64,128]{4,3,2,1,0:T(8,128)(2,1)}) custom-call(s32[8,8]{1,0:T(8,128)} %shift_ref.1, bf16[2048,4,128]{2,1,0:T(4,128)(2,1)} %k_hbm.1, bf16[2048,4,128]{2,1,0:T(4,128)(2,1)} %v_hbm.1), custom_call_target="tpu_custom_call" | custom-call | tf_op jit(solution)/shard_map/gather_summaries/pallas_call | solution.py:44
  3.2 0.0 copy-start.9
  3.3 0.0 copy-start
  3.3 26.1 %all_to_all.20.km_ref.vm_ref = bf16[8,2,2,64,128]{4,3,2,1,0:T(8,128)(2,1)S(1)} all-to-all(bf16[8,2,2,64,128]{4,3,2,1,0:T(8,128)(2,1)} %get-tuple-element.19), channel_id=1, replica_groups=mesh['x_lo'=2,'z'=8,'core'=2,'x_hi'=2,'y'=4] {'z'}, dimensions={0} | all-to-all | bytes 1048576 | tf_op jit(solution)/shard_map/all_to_all | solution.py:248
  29.4 3.5 %all-to-all-start.1 = ((bf16[8,2,2,64,128]{4,3,2,1,0:T(8,128)(2,1)}), bf16[8,2,2,64,128]{4,3,2,1,0:T(8,128)(2,1)S(1)}, u32[]{:S(2)}, u32[]{:S(2)}) async-start(bf16[8,2,2,64,128]{4,3,2,1,0:T(8,128)(2,1)} %get-tuple-element.20), calls=%async_computation.1 | async-start | bytes 1048576 | tf_op jit(solution)/shard_map/all_to_all | solution.py:248
  32.9 0.0 copy-done.8
  32.9 0.0 copy-done.9
  32.9 0.1 copy.7.heat_ref
  33.0 0.0 copy-done
  33.0 0.0 copy-start.1
  33.0 1.6 %copy-done.1 = bf16[2048,4,128]{2,1,0:T(4,128)(2,1)S(1)} copy-done((bf16[2048,4,128]{2,1,0:T(4,128)(2,1)S(1)}, bf16[2048,4,128]{2,1,0:T(4,128)(2,1)}, u32[]{:S(2)}) %copy-start.1) | copy-done | bytes 2097176
  34.6 0.0 copy-start.2
  34.6 1.6 %copy-done.2 = bf16[2048,4,128]{2,1,0:T(4,128)(2,1)S(1)} copy-done((bf16[2048,4,128]{2,1,0:T(4,128)(2,1)S(1)}, bf16[2048,4,128]{2,1,0:T(4,128)(2,1)}, u32[]{:S(2)}) %copy-start.2) | copy-done | bytes 2097176
  36.2 9.9 %band.1 = (bf16[4,2048,256]{2,1,0:T(8,128)(2,1)S(1)}, f32[4,2048,128]{2,1,0:T(8,128)S(1)}, f32[4,2048,128]{2,1,0:T(8,128)S(1)}) custom-call(f32[8,1]{1,0:T(8,128)S(1)} %copy.7.heat_ref, s32[8,256]{1,0:T(8,128)S(1)} %reshape.19.place_ref, bf16[8192,128]{1,0:T(8,128)(2,1)S(1)} %bitcast.11, bf16[8192,128]{1,0:T(8,128)(2,1)S(1)} %bitcast.9, ...), custom_call_target="tpu_custom_call" | custom-call | flops 2147483648 | bytes 20971520 | tf_op jit(solution)/shard_map/band/pallas_call | solution.py:122
  46.1 0.0 copy-start.3
  46.1 1.9 %copy-done.3 = bf16[4,2048,256]{2,1,0:T(8,128)(2,1)} copy-done((bf16[4,2048,256]{2,1,0:T(8,128)(2,1)}, bf16[4,2048,256]{2,1,0:T(8,128)(2,1)S(1)}, u32[]{:S(2)}) %copy-start.3) | copy-done | bytes 4194328
  48.0 0.0 copy-start.4
  48.0 2.0 %copy-done.4 = f32[4,2048,128]{2,1,0:T(8,128)} copy-done((f32[4,2048,128]{2,1,0:T(8,128)}, f32[4,2048,128]{2,1,0:T(8,128)S(1)}, u32[]{:S(2)}) %copy-start.4) | copy-done | bytes 4194328
  50.0 0.0 copy-start.5
  50.0 2.0 %copy-done.5 = f32[4,2048,128]{2,1,0:T(8,128)} copy-done((f32[4,2048,128]{2,1,0:T(8,128)}, f32[4,2048,128]{2,1,0:T(8,128)S(1)}, u32[]{:S(2)}) %copy-start.5) | copy-done | bytes 4194328
  52.0 0.0 all-to-all-done.1.km_ref.vm_ref
  52.0 1.3 collective-permute-start.3
  53.3 1.3 collective-permute-start
  54.6 0.1 collective-permute-start.5
  54.7 14.1 %collective-permute-done.3.km_ref.vm_ref = bf16[8,2,2,64,128]{4,3,2,1,0:T(8,128)(2,1)S(1)} collective-permute-done((bf16[8,2,2,64,128]{4,3,2,1,0:T(8,128)(2,1)S(1)}, bf16[8,2,2,64,128]{4,3,2,1,0:T(8,128)(2,1)S(1)}, u32[]{:S(2)}, u32[]{:S(2)}) %collective-permute-start.3) | collective-permute-done | bytes 524320 | tf_op jit(solution)/shard_map/ppermute | solution.py:257
  68.7 0.0 collective-permute-start.4
  68.8 0.1 pad_add_fusion.at_ref
  68.8 0.5 collective-permute-start.2
  69.4 7.6 %collective-permute-done.km_ref.vm_ref = bf16[8,2,2,64,128]{4,3,2,1,0:T(8,128)(2,1)S(1)} collective-permute-done((bf16[8,2,2,64,128]{4,3,2,1,0:T(8,128)(2,1)S(1)}, bf16[8,2,2,64,128]{4,3,2,1,0:T(8,128)(2,1)S(1)}, u32[]{:S(2)}, u32[]{:S(2)}) %collective-permute-start) | collective-permute-done | bytes 524320 | tf_op jit(solution)/shard_map/ppermute | solution.py:257
  77.0 0.0 collective-permute-start.1
  77.0 0.0 collective-permute-done.5.ko_ref.vo_ref
  77.0 8.3 %own_1.1 = (f32[2,2048,128]{2,1,0:T(8,128)S(1)}, f32[2,2048,128]{2,1,0:T(8,128)S(1)}) custom-call(s32[3]{0:T(128)S(1)} %pad_add_fusion.at_ref, bf16[4,2048,256]{2,1,0:T(8,128)(2,1)} %copy-done.3, bf16[8,2,2,64,128]{4,3,2,1,0:T(8,128)(2,1)S(1)} %all-to-all-done.1.km_ref.vm_ref, bf16[8,2,2,64,128]{4,3,2,1,0:T(8,128)(2,1)S(1)} %collective-permute-done.5.ko_ref.vo_ref, ...), custom_call_target="tpu_custom_call" | custom-call | flops 4294967296 | bytes 12582912 | tf_op jit(solution)/shard_map/own_1/pallas_call | solution.py:182
  85.3 0.0 copy-start.7
  85.3 1.3 copy-done.7
  86.6 0.0 collective-permute-done.4.ko_ref.vo_ref
  86.6 8.8 %far_1.1 = bf16[8,2,256,128]{3,2,1,0:T(8,128)(2,1)} custom-call(s32[3]{0:T(128)S(1)} %pad_add_fusion.at_ref, bf16[4,2048,256]{2,1,0:T(8,128)(2,1)} %copy-done.3, bf16[8,2,2,64,128]{4,3,2,1,0:T(8,128)(2,1)S(1)} %collective-permute-done.3.km_ref.vm_ref, bf16[8,2,2,64,128]{4,3,2,1,0:T(8,128)(2,1)} %collective-permute-done.4.ko_ref.vo_ref, ...), custom_call_target="tpu_custom_call" | custom-call | flops 4294967296 | bytes 12582912 | tf_op jit(solution)/shard_map/far_1/pallas_call | solution.py:182
  95.4 6.0 %all-to-all-start.3 = ((bf16[8,2,256,128]{3,2,1,0:T(8,128)(2,1)}), bf16[8,2,256,128]{3,2,1,0:T(8,128)(2,1)}, u32[]{:S(2)}, u32[]{:S(2)}) async-start(bf16[8,2,256,128]{3,2,1,0:T(8,128)(2,1)} %far_1.1), calls=%async_computation.3 | async-start | bytes 2097152 | tf_op jit(solution)/shard_map/all_to_all | solution.py:261
  101.5 0.0 collective-permute-done.2.ko_ref.vo_ref
  101.5 8.3 %own_0.1 = (f32[2,2048,128]{2,1,0:T(8,128)S(1)}, f32[2,2048,128]{2,1,0:T(8,128)S(1)}) custom-call(s32[3]{0:T(128)S(1)} %pad_add_fusion.at_ref, bf16[4,2048,256]{2,1,0:T(8,128)(2,1)} %copy-done.3, bf16[8,2,2,64,128]{4,3,2,1,0:T(8,128)(2,1)S(1)} %all_to_all.20.km_ref.vm_ref, bf16[8,2,2,64,128]{4,3,2,1,0:T(8,128)(2,1)} %collective-permute-done.2.ko_ref.vo_ref, ...), custom_call_target="tpu_custom_call" | custom-call | flops 4294967296 | bytes 12582912 | tf_op jit(solution)/shard_map/own_0/pallas_call | solution.py:182
  109.8 0.0 copy-start.6
  109.8 1.3 copy-done.6
  111.1 0.0 collective-permute-done.1.ko_ref.vo_ref
  111.1 8.2 %far_0.1 = bf16[8,2,256,128]{3,2,1,0:T(8,128)(2,1)S(1)} custom-call(s32[3]{0:T(128)S(1)} %pad_add_fusion.at_ref, bf16[4,2048,256]{2,1,0:T(8,128)(2,1)} %copy-done.3, bf16[8,2,2,64,128]{4,3,2,1,0:T(8,128)(2,1)S(1)} %collective-permute-done.km_ref.vm_ref, bf16[8,2,2,64,128]{4,3,2,1,0:T(8,128)(2,1)} %collective-permute-done.1.ko_ref.vo_ref, ...), custom_call_target="tpu_custom_call" | custom-call | flops 4294967296 | bytes 12582912 | tf_op jit(solution)/shard_map/far_0/pallas_call | solution.py:182
  119.3 0.0 all-to-all-done.3.x1_ref
  119.3 24.4 %all_to_all.21.x0_ref = bf16[8,2,256,128]{3,2,1,0:T(8,128)(2,1)} all-to-all(bf16[8,2,256,128]{3,2,1,0:T(8,128)(2,1)S(1)} %far_0.1), channel_id=1, replica_groups=mesh['x_lo'=2,'z'=8,'core'=2,'x_hi'=2,'y'=4] {'x_hi','y'}, dimensions={0} | all-to-all | bytes 2097152 | tf_op jit(solution)/shard_map/all_to_all | solution.py:261
  143.8 6.4 %assemble.1 = bf16[8192,128]{1,0:T(8,128)(2,1)} custom-call(bf16[8,2,256,128]{3,2,1,0:T(8,128)(2,1)} %all_to_all.21.x0_ref, bf16[8,2,256,128]{3,2,1,0:T(8,128)(2,1)} %all-to-all-done.3.x1_ref), custom_call_target="tpu_custom_call" | custom-call | tf_op jit(solution)/shard_map/assemble/pallas_call | solution.py:233
  (2 shorter events, 0.0 us)
Async XLA Ops:
  0.0 32.9 %copy-start.8 = (s32[2048]{0:T(1024)S(1)}, s32[2048]{0:T(1024)}, u32[]{:S(2)}) copy-start(s32[2048]{0:T(1024)} %param.10) | copy-start | bytes 24580
  3.2 29.6 %copy-start.9 = (f32[4]{0:T(128)S(1)}, f32[4]{0:T(128)}, u32[]{:S(2)}) copy-start(f32[4]{0:T(128)} %param.9) | copy-start | bytes 52
  3.3 29.7 %copy-start = (bf16[2048,4,128]{2,1,0:T(4,128)(2,1)S(1)}, bf16[2048,4,128]{2,1,0:T(4,128)(2,1)}, u32[]{:S(2)}) copy-start(bf16[2048,4,128]{2,1,0:T(4,128)(2,1)} %k_hbm.1) | copy-start | bytes 6291460
  29.4 22.6 %all-to-all-start.1 = ((bf16[8,2,2,64,128]{4,3,2,1,0:T(8,128)(2,1)}), bf16[8,2,2,64,128]{4,3,2,1,0:T(8,128)(2,1)S(1)}, u32[]{:S(2)}, u32[]{:S(2)}) async-start(bf16[8,2,2,64,128]{4,3,2,1,0:T(8,128)(2,1)} %get-tuple-element.20), calls=%async_computation.1 | async-start | bytes 1048576 | tf_op jit(solution)/shard_map/all_to_all | solution.py:248
  33.0 1.6 %copy-start.1 = (bf16[2048,4,128]{2,1,0:T(4,128)(2,1)S(1)}, bf16[2048,4,128]{2,1,0:T(4,128)(2,1)}, u32[]{:S(2)}) copy-start(bf16[2048,4,128]{2,1,0:T(4,128)(2,1)} %v_hbm.1) | copy-start | bytes 6291460
  34.6 1.6 %copy-start.2 = (bf16[2048,4,128]{2,1,0:T(4,128)(2,1)S(1)}, bf16[2048,4,128]{2,1,0:T(4,128)(2,1)}, u32[]{:S(2)}) copy-start(bf16[2048,4,128]{2,1,0:T(4,128)(2,1)} %param.6) | copy-start | bytes 6291460
  46.1 1.9 %copy-start.3 = (bf16[4,2048,256]{2,1,0:T(8,128)(2,1)}, bf16[4,2048,256]{2,1,0:T(8,128)(2,1)S(1)}, u32[]{:S(2)}) copy-start(bf16[4,2048,256]{2,1,0:T(8,128)(2,1)S(1)} %get-tuple-element.24.q_ref) | copy-start | bytes 12582916
  48.0 2.0 %copy-start.4 = (f32[4,2048,128]{2,1,0:T(8,128)}, f32[4,2048,128]{2,1,0:T(8,128)S(1)}, u32[]{:S(2)}) copy-start(f32[4,2048,128]{2,1,0:T(8,128)S(1)} %get-tuple-element.26.acc_ref) | copy-start | bytes 12582916
  50.0 2.0 %copy-start.5 = (f32[4,2048,128]{2,1,0:T(8,128)}, f32[4,2048,128]{2,1,0:T(8,128)S(1)}, u32[]{:S(2)}) copy-start(f32[4,2048,128]{2,1,0:T(8,128)S(1)} %get-tuple-element.27.ml_ref) | copy-start | bytes 12582916
  52.0 16.7 %collective-permute-start.3 = (bf16[8,2,2,64,128]{4,3,2,1,0:T(8,128)(2,1)S(1)}, bf16[8,2,2,64,128]{4,3,2,1,0:T(8,128)(2,1)S(1)}, u32[]{:S(2)}, u32[]{:S(2)}) collective-permute-start(bf16[8,2,2,64,128]{4,3,2,1,0:T(8,128)(2,1)S(1)} %all-to-all-done.1.km_ref.vm_ref), channel_id=1, source_target_pairs={{0,128},{1,129},{2,130},{3,131},{4,132},{5,133},{6,134},{7,135},{8... | collective-permute-start | bytes 1572872 | tf_op jit(solution)/shard_map/ppermute | solution.py:257
  53.3 23.7 %collective-permute-start = (bf16[8,2,2,64,128]{4,3,2,1,0:T(8,128)(2,1)S(1)}, bf16[8,2,2,64,128]{4,3,2,1,0:T(8,128)(2,1)S(1)}, u32[]{:S(2)}, u32[]{:S(2)}) collective-permute-start(bf16[8,2,2,64,128]{4,3,2,1,0:T(8,128)(2,1)S(1)} %all_to_all.20.km_ref.vm_ref), channel_id=1, source_target_pairs={{0,128},{1,129},{2,130},{3,131},{4,132},{5,133},{6,134},{7,135},{8... | collective-permute-start | bytes 1572872 | tf_op jit(solution)/shard_map/ppermute | solution.py:257
  54.6 22.4 %collective-permute-start.5 = (bf16[8,2,2,64,128]{4,3,2,1,0:T(8,128)(2,1)S(1)}, bf16[8,2,2,64,128]{4,3,2,1,0:T(8,128)(2,1)S(1)}, u32[]{:S(2)}, u32[]{:S(2)}) collective-permute-start(bf16[8,2,2,64,128]{4,3,2,1,0:T(8,128)(2,1)S(1)} %all-to-all-done.1.km_ref.vm_ref), channel_id=1, source_target_pairs={{0,8},{8,0},{1,9},{9,1},{2,10},{10,2},{3,11},{11,3},{4,12},{12,4},... | collective-permute-start | bytes 1572872 | tf_op jit(solution)/shard_map/ppermute | solution.py:256
  68.7 17.9 %collective-permute-start.4 = (bf16[8,2,2,64,128]{4,3,2,1,0:T(8,128)(2,1)S(1)}, bf16[8,2,2,64,128]{4,3,2,1,0:T(8,128)(2,1)}, u32[]{:S(2)}, u32[]{:S(2)}) collective-permute-start(bf16[8,2,2,64,128]{4,3,2,1,0:T(8,128)(2,1)S(1)} %collective-permute-done.3.km_ref.vm_ref), channel_id=1, source_target_pairs={{0,8},{8,0},{1,9},{9,1},{2,10},{10,2},{3,11},{11,3},{4,12},{12,4},... | collective-permute-start | bytes 1572872 | tf_op jit(solution)/shard_map/ppermute | solution.py:258
  68.8 32.7 %collective-permute-start.2 = (bf16[8,2,2,64,128]{4,3,2,1,0:T(8,128)(2,1)S(1)}, bf16[8,2,2,64,128]{4,3,2,1,0:T(8,128)(2,1)}, u32[]{:S(2)}, u32[]{:S(2)}) collective-permute-start(bf16[8,2,2,64,128]{4,3,2,1,0:T(8,128)(2,1)S(1)} %all_to_all.20.km_ref.vm_ref), channel_id=1, source_target_pairs={{0,8},{8,0},{1,9},{9,1},{2,10},{10,2},{3,11},{11,3},{4,12},{12,4},... | collective-permute-start | bytes 1572872 | tf_op jit(solution)/shard_map/ppermute | solution.py:256
  77.0 34.1 %collective-permute-start.1 = (bf16[8,2,2,64,128]{4,3,2,1,0:T(8,128)(2,1)S(1)}, bf16[8,2,2,64,128]{4,3,2,1,0:T(8,128)(2,1)}, u32[]{:S(2)}, u32[]{:S(2)}) collective-permute-start(bf16[8,2,2,64,128]{4,3,2,1,0:T(8,128)(2,1)S(1)} %collective-permute-done.km_ref.vm_ref), channel_id=1, source_target_pairs={{0,8},{8,0},{1,9},{9,1},{2,10},{10,2},{3,11},{11,3},{4,12},{12,4},... | collective-permute-start | bytes 1572872 | tf_op jit(solution)/shard_map/ppermute | solution.py:258
  85.3 1.3 copy-start.7
  95.4 23.9 %all-to-all-start.3 = ((bf16[8,2,256,128]{3,2,1,0:T(8,128)(2,1)}), bf16[8,2,256,128]{3,2,1,0:T(8,128)(2,1)}, u32[]{:S(2)}, u32[]{:S(2)}) async-start(bf16[8,2,256,128]{3,2,1,0:T(8,128)(2,1)} %far_1.1), calls=%async_computation.3 | async-start | bytes 2097152 | tf_op jit(solution)/shard_map/all_to_all | solution.py:261
  109.8 1.3 copy-start.6

commit v2 on v1

v2 whole, which is shorter than its diff:
```python
import functools
import math

import jax
import jax.numpy as jnp
from jax import lax
from jax.experimental import pallas as pl
from jax.experimental.pallas import tpu as pltpu
from jax.sharding import Mesh
from jax.sharding import PartitionSpec as P

F32, BF16 = jnp.float32, jnp.bfloat16
NEG = -1e30
STRIDE, SUMM, DIM, HEADS = 256, 8, 128, 4
BLOCKS = 8
COLS = BLOCKS * SUMM
CHIPS = 8
GROUP = 2
TRANS_B = (((1,), (1,)), ((), ()))
CTX = ("x_lo", "z", "core")
HEAD = ("x_hi", "y")


def gather_kernel(shift_ref, k_hbm, v_hbm, out0_ref, out1_ref, rows_ref, wide_ref, sems):
    for w, hbm in enumerate((k_hbm, v_hbm)):
        for c in range(COLS):
            row = (c // SUMM) * STRIDE + shift_ref[c // SUMM, c % SUMM]
            pltpu.make_async_copy(
                hbm.at[pl.ds(row, 1)], rows_ref.at[w, pl.ds(c, 1)], sems.at[w]
            ).start()
    for w, hbm in enumerate((k_hbm, v_hbm)):
        pltpu.make_async_copy(hbm.at[pl.ds(0, COLS)], rows_ref.at[w], sems.at[w]).wait()
        for c in range(COLS):
            wide_ref[w, pl.ds(c * HEADS, HEADS), :] = rows_ref[w, c].astype(F32)
        for h in range(HEADS):
            out_ref = (out0_ref, out1_ref)[h // GROUP]
            x = wide_ref[w, pl.ds(h, COLS, stride=HEADS), :].astype(BF16)
            for d in range(CHIPS):
                out_ref[d, w, h % GROUP] = x


def gather_summaries(digest_shifts, keys, values):
    out = jax.ShapeDtypeStruct((CHIPS, 2, GROUP, COLS, DIM), BF16)
    return pl.pallas_call(
        gather_kernel,
        in_specs=[
            pl.BlockSpec(memory_space=pltpu.SMEM),
            pl.BlockSpec(memory_space=pl.ANY),
            pl.BlockSpec(memory_space=pl.ANY),
        ],
        out_shape=[out, out],
        scratch_shapes=[
            pltpu.VMEM((2, COLS, HEADS, DIM), BF16),
            pltpu.VMEM((2, COLS * HEADS, DIM), F32),
            pltpu.SemaphoreType.DMA((2,)),
        ],
        name="gather_summaries",
    )(digest_shifts, keys, values)


def attend(q, keys, values, biases, m, l, acc):
    scores = []
    for k, bias in zip(keys, biases):
        s = lax.dot_general(
            q, jnp.concatenate([k, k], axis=1), TRANS_B, preferred_element_type=F32
        )
        scores.append(s if bias is None else s + bias)
    top = m
    for s in scores:
        peak = s.max(axis=1, keepdims=True)
        top = peak if top is None else jnp.maximum(top, peak)
    if m is not None:
        shrink = jnp.exp2(m - top)
        acc, l = acc * shrink, l * shrink
    for s, v in zip(scores, values):
        p = jnp.exp2(s - top).astype(BF16)
        o = jnp.dot(
            p, jnp.concatenate([v, jnp.ones_like(v)], axis=1), preferred_element_type=F32
        )
        acc = o[:, :DIM] if acc is None else acc + o[:, :DIM]
        l = o[:, DIM:] if l is None else l + o[:, DIM:]
    return top, l, acc


def pack_stats(m, l):
    lane = lax.broadcasted_iota(jnp.int32, l.shape, 1)
    return jnp.where(lane < DIM // 2, m, l)


def unpack_stats(ml):
    return ml[:, 0:1], jnp.broadcast_to(ml[:, DIM // 2 : DIM // 2 + 1], ml.shape)


def band_kernel(heat_ref, place_ref, q_ref, k_ref, v_ref, *refs):
    *outs, wide_ref = refs
    j = pl.program_id(0)
    place = place_ref[pl.ds(j, 1), :].astype(F32)
    log_place = jnp.broadcast_to(jnp.log(1.0 + place), (8, STRIDE))
    scale = (1.0 + heat_ref[...] * log_place) * (math.log2(math.e) / math.sqrt(DIM))
    scale = scale.T
    for w, ref in enumerate((q_ref, k_ref, v_ref)):
        wide_ref[w] = ref[...].astype(F32)
    inner = [lax.broadcasted_iota(jnp.int32, (STRIDE, STRIDE), d) for d in range(2)]
    bias = jnp.where(inner[0] >= inner[1], 0.0, NEG)
    for h in range(HEADS):
        q, k, v = (wide_ref[w, pl.ds(h, STRIDE, stride=HEADS), :] for w in range(3))
        q = q * scale[:, h : h + 1]
        high = q.astype(BF16)
        low = (q - high.astype(F32)).astype(BF16)
        q = jnp.concatenate([high, low], axis=1)
        m, l, acc = attend(q, (k.astype(BF16),), (v.astype(BF16),), (bias,), None, None, None)
        qs_ref, acc_ref, ml_ref = outs[3 * (h // GROUP) :][:3]
        qs_ref[h % GROUP] = q
        acc_ref[h % GROUP] = acc
        ml_ref[h % GROUP] = pack_stats(m, l)


def band(heat, places, q, k, v):
    tokens = BLOCKS * STRIDE
    whole = lambda *s: pl.BlockSpec(s, lambda j: (0,) * len(s))
    rows = pl.BlockSpec((STRIDE * HEADS, DIM), lambda j: (j, 0))
    out = lambda d: pl.BlockSpec((GROUP, STRIDE, d), lambda j: (0, j, 0))
    shape = lambda d, t: jax.ShapeDtypeStruct((GROUP, tokens, d), t)
    return pl.pallas_call(
        band_kernel,
        grid=(BLOCKS,),
        in_specs=[whole(8, 1), whole(BLOCKS, STRIDE), rows, rows, rows],
        out_specs=[out(2 * DIM), out(DIM), out(DIM)] * 2,
        out_shape=[shape(2 * DIM, BF16), shape(DIM, F32), shape(DIM, F32)] * 2,
        scratch_shapes=[pltpu.VMEM((3, STRIDE * HEADS, DIM), F32)],
        compiler_params=pltpu.CompilerParams(vmem_limit_bytes=60 << 20),
        cost_estimate=pl.CostEstimate(
            flops=4 * HEADS * tokens * STRIDE * DIM * 2, bytes_accessed=20 << 20,
            transcendentals=HEADS * tokens * STRIDE,
        ),
        name="band",
    )(heat, places, q, k, v)


def attend_blocks(q_ref, kv_refs, biases, acc_ref, ml_ref, put):
    flat = lambda ref: ref[...].reshape(CHIPS * COLS, DIM)
    keys = [flat(k) for k, _ in kv_refs]
    values = [flat(v) for _, v in kv_refs]
    for j in range(BLOCKS):
        rows = pl.ds(j * STRIDE, STRIDE)
        m, l = unpack_stats(ml_ref[0, rows, :])
        put(j, *attend(q_ref[0, rows, :], keys, values, biases(j), m, l, acc_ref[0, rows, :]))


def own_biases(at_ref):
    z, core = at_ref[1], at_ref[2]
    col = lax.broadcasted_iota(jnp.int32, (1, CHIPS * COLS), 1)
    other = jnp.where(col < (z + core) * COLS, 0.0, NEG)
    return lambda j: [jnp.where(col < z * COLS + SUMM * j, 0.0, NEG), other]


def no_biases(j):
    return [None, None]


def summary_kernel(own, far, at_ref, q_ref, *refs):
    kv_refs, refs = refs[: 4 * (own + far)], refs[4 * (own + far) :]
    acc_ref, ml_ref, *outs = refs
    kv = [(kv_refs[i], kv_refs[i + 2]) for s in range(own + far) for i in (4 * s, 4 * s + 1)]

    def keep(j, m, l, acc):
        rows = pl.ds(j * STRIDE, STRIDE)
        outs[0][0, rows, :] = acc
        outs[1][0, rows, :] = pack_stats(m, l)

    def finish(j, m, l, acc):
        outs[0][j, 0] = (acc / l).astype(BF16)

    if not far:
        attend_blocks(q_ref, kv, own_biases(at_ref), acc_ref, ml_ref, keep)
        return

    @pl.when(at_ref[0] == 1)
    def _():
        near = own_biases(at_ref) if own else lambda j: []
        attend_blocks(q_ref, kv, lambda j: near(j) + [None, None], acc_ref, ml_ref, finish)

    @pl.when(at_ref[0] == 0)
    def _():
        if own:
            attend_blocks(q_ref, kv[:2], own_biases(at_ref), acc_ref, ml_ref, finish)
        else:
            for j in range(BLOCKS):
                rows = pl.ds(j * STRIDE, STRIDE)
                m, l = unpack_stats(ml_ref[0, rows, :])
                finish(j, m, l, acc_ref[0, rows, :])


def summaries(at, q, acc, ml, own=(), far=()):
    tokens = BLOCKS * STRIDE
    kv = lambda w: pl.BlockSpec((CHIPS, 1, 1, COLS, DIM), lambda h: (0, w, h, 0, 0))
    state = lambda d: pl.BlockSpec((1, tokens, d), lambda h: (h, 0, 0))
    sets = [s for s in (own, far) if s]
    if far:
        out_specs = pl.BlockSpec((BLOCKS, 1, STRIDE, DIM), lambda h: (0, h, 0, 0))
        out_shape = jax.ShapeDtypeStruct((BLOCKS, GROUP, STRIDE, DIM), BF16)
    else:
        out_specs = [state(DIM)] * 2
        out_shape = [jax.ShapeDtypeStruct((GROUP, tokens, DIM), F32)] * 2
    work = GROUP * tokens * 2 * CHIPS * COLS * len(sets)
    return pl.pallas_call(
        functools.partial(summary_kernel, bool(own), bool(far)),
        grid=(GROUP,),
        in_specs=[
            pl.BlockSpec(memory_space=pltpu.SMEM),
            state(2 * DIM),
            *[kv(0), kv(0), kv(1), kv(1)] * len(sets),
            state(DIM), state(DIM),
        ],
        out_specs=out_specs,
        out_shape=out_shape,
        compiler_params=pltpu.CompilerParams(vmem_limit_bytes=60 << 20),
        cost_estimate=pl.CostEstimate(
            flops=8 * work * DIM, bytes_accessed=12 << 20, transcendentals=work
        ),
        name="_".join(n for n, s in (("own", own), ("far", far)) if s),
    )(at, q, *[x for mine, other in sets for x in (mine, other) * 2], acc, ml)


def assemble_kernel(x0_ref, x1_ref, out_ref):
    heads = [(x0_ref, x1_ref)[h // GROUP][s, h % GROUP] for s in range(BLOCKS) for h in range(HEADS)]
    out_ref[...] = jnp.swapaxes(jnp.stack(heads), 0, 1)


def assemble(x0, x1, steps=4):
    count = STRIDE // steps
    total = BLOCKS * HEADS
    spec = pl.BlockSpec((BLOCKS, GROUP, count, DIM), lambda t: (0, 0, t, 0))
    return pl.pallas_call(
        assemble_kernel,
        grid=(steps,),
        in_specs=[spec, spec],
        out_specs=pl.BlockSpec((count, total, DIM), lambda t: (t, 0, 0)),
        out_shape=jax.ShapeDtypeStruct((STRIDE, total, DIM), BF16),
        compiler_params=pltpu.CompilerParams(vmem_limit_bytes=60 << 20),
        name="assemble",
    )(x0, x1)


def after(value, *done):
    return lax.optimization_barrier((value, *done))[0]


def per_device(q, k, v, heat, places, shifts):
    at = jnp.stack([lax.axis_index(a) for a in CTX]).astype(jnp.int32)
    tokens = BLOCKS * STRIDE
    swap, up = [(0, 1), (1, 0)], [(0, 1)]
    flat = lambda x: x.reshape(tokens * HEADS, DIM)
    spread = lambda x: lax.all_to_all(x, "z", 0, 0, tiled=True)
    give = lambda x: lax.all_to_all(x, HEAD, 0, 0, tiled=True)
    heat8 = jnp.pad(heat, (0, 8 - HEADS)).reshape(8, 1)

    send0, send1 = gather_summaries(shifts, k, v)
    mine0 = spread(send0)
    qs0, acc0, ml0, qs1, acc1, ml1 = band(heat8, places.reshape(BLOCKS, STRIDE), flat(q), flat(k), flat(v))
    mine0 = after(mine0, ml0)
    mine1 = spread(after(send1, mine0))
    other0 = lax.ppermute(mine0, "core", swap)
    far0 = lax.ppermute(mine0, "x_lo", up)
    state0 = summaries(at, qs0, acc0, ml0, own=(mine0, other0))
    far0 = after(far0, state0[1])
    far_other0 = lax.ppermute(far0, "core", swap)
    mine1 = after(mine1, state0[1])
    other1 = lax.ppermute(mine1, "core", swap)
    far1 = lax.ppermute(mine1, "x_lo", up)
    part0 = summaries(at, qs0, *state0, far=(far0, far_other0))
    out0 = give(part0)
    far1 = after(far1, part0)
    far_other1 = lax.ppermute(far1, "core", swap)
    acc1 = after(acc1, part0)
    part1 = summaries(at, qs1, acc1, ml1, own=(mine1, other1), far=(far1, far_other1))
    out1 = give(after(part1, out0))
    return assemble(out0, out1)


def solution(mesh):
    devices = mesh.devices
    wide = Mesh(devices.reshape(2, 8, 2, 2, 4), CTX + HEAD)
    in_specs = (
        P(CTX, HEAD, None),
        P(CTX, HEAD, None),
        P(CTX, HEAD, None),
        P(HEAD),
        P(CTX),
        P(CTX, None),
    )
    return jax.shard_map(
        per_device, mesh=wide, in_specs=in_specs, out_specs=P(CTX + HEAD, None, None),
        check_vma=False,
    )
```

time: 151 us -> 120 us (0.79)
  blocking collectives: 50.5 us -> 23.6 us
  starting transfers between devices: 12.7 us -> 21.9 us
  local copies, waits for them, and re-layouts: 11.8 us -> 3.91 us
  waiting for transfers between devices: 21.7 us -> 14.8 us
    all_to_all x2 -> x1, blocking collectives: 50.5 us -> 23.6 us  [per_device(): give = lambda x: lax.all_to_all(x, HEAD, 0, 0, tiled=True)]
    ppermute x6, waiting for transfers between devices: 21.7 us -> 4.28 us  [the longest x1 4.27 us: per_device(): far1 = lax.ppermute(mine1, 'x_lo', up)]
    all_to_all x2 -> x3, waiting for transfers between devices: 0.01 us -> 10.6 us  [the longest x2 9.51 us: per_device(): spread = lambda x: lax.all_to_all(x, 'z', 0, 0, tiled=True)]
    all_to_all x2 -> x3, starting transfers between devices: 9.53 us -> 18.9 us  [the longest x2 12.9 us: per_device(): spread = lambda x: lax.all_to_all(x, 'z', 0, 0, tiled=True)]
    unnamed x20 -> x22, local copies, waits for them, and re-layouts: 11.7 us -> 2.65 us
    pallas_call x1, Pallas kernels: 9.9 us -> 13.3 us  [band(): pl.pallas_call(band_kernel, grid=(BLOCKS,), in_specs=[whole(8, 1), whole(...]
    pallas_call x1, Pallas kernels: 6.36 us -> 4.03 us  [assemble(): pl.pallas_call(assemble_kernel, grid=(steps,), in_specs=[spec, spec], out...]
    pallas_call x4 -> x3, Pallas kernels: 33.6 us -> 33.3 us  [summaries(): pl.pallas_call(functools.partial(summary_kernel, bool(own), bool(far)), g...]
  transfers between devices with their start and end apart: 8 -> 9, of which waited for: 2 -> 4; matrix products, arithmetic and copies ran while one was open for 0% -> 2% of each run, Pallas kernels for 29% -> 39%
where the time goes in v2:
time: 120 us; the launch traced here: 119 us
  Pallas kernels  53.7 us (45%)
  blocking collectives  23.6 us (20%)
  starting transfers between devices  21.9 us (18%)
  waiting for transfers between devices  14.8 us (12%)
  local copies, waits for them, and re-layouts  3.91 us (3%)
    pallas_call x3, Pallas kernels, summaries(): pl.pallas_call(functools.partial(summary_kernel, bool(own), bool(far)), g...  33.3 us
    all_to_all x1, blocking collectives, per_device(): give = lambda x: lax.all_to_all(x, HEAD, 0, 0, tiled=True)  23.6 us
    pallas_call x1, Pallas kernels, band(): pl.pallas_call(band_kernel, grid=(BLOCKS,), in_specs=[whole(8, 1), whole(...  13.3 us
    all_to_all x2, starting transfers between devices, per_device(): spread = lambda x: lax.all_to_all(x, 'z', 0, 0, tiled=True)  12.9 us
    all_to_all x2, waiting for transfers between devices, per_device(): spread = lambda x: lax.all_to_all(x, 'z', 0, 0, tiled=True)  9.51 us
    all_to_all x1, starting transfers between devices, per_device(): give = lambda x: lax.all_to_all(x, HEAD, 0, 0, tiled=True)  6.04 us
    ppermute x1, waiting for transfers between devices, per_device(): far1 = lax.ppermute(mine1, 'x_lo', up)  4.27 us
    pallas_call x1, Pallas kernels, assemble(): pl.pallas_call(assemble_kernel, grid=(steps,), in_specs=[spec, spec], out...  4.03 us
  transfers between devices with their start and end apart: 9, of which 4 were waited for; matrix products, arithmetic and copies ran while one was open for 2% of the time, Pallas kernels for 39%

profile of v2, /device:TPU:2, one launch (start us, length us, event | category | flops | bytes accessed | tf_op | source)
XLA Modules:
  0.0 118.8 jit_solution(2969984052338049466)
XLA Ops:
  0.0 0.0 copy-start.10
  0.0 0.0 copy-start.3
  0.0 3.2 %gather_summaries.1 = (bf16[8,2,2,64,128]{4,3,2,1,0:T(8,128)(2,1)}, bf16[8,2,2,64,128]{4,3,2,1,0:T(8,128)(2,1)}) custom-call(s32[8,8]{1,0:T(8,128)} %shift_ref.1, bf16[2048,4,128]{2,1,0:T(4,128)(2,1)} %k_hbm.1, bf16[2048,4,128]{2,1,0:T(4,128)(2,1)} %v_hbm.1), custom_call_target="tpu_custom_call" | custom-call | tf_op jit(solution)/shard_map/gather_summaries/pallas_call | solution.py:44
  3.2 8.5 %all-to-all-start = ((bf16[8,2,2,64,128]{4,3,2,1,0:T(8,128)(2,1)}), bf16[8,2,2,64,128]{4,3,2,1,0:T(8,128)(2,1)S(1)}, u32[]{:S(2)}, u32[]{:S(2)}) async-start(bf16[8,2,2,64,128]{4,3,2,1,0:T(8,128)(2,1)} %get-tuple-element.23), calls=%async_computation | async-start | bytes 1048576 | tf_op jit(solution)/shard_map/all_to_all | solution.py:254
  11.6 0.0 copy-done.10
  11.7 0.7 copy.7.heat_ref
  12.3 0.0 copy-done.3
  12.3 0.6 reshape.16.place_ref
  12.9 13.3 %band.1 = (bf16[2,2048,256]{2,1,0:T(8,128)(2,1)}, f32[2,2048,128]{2,1,0:T(8,128)}, f32[2,2048,128]{2,1,0:T(8,128)}, bf16[2,2048,256]{2,1,0:T(8,128)(2,1)}, f32[2...) custom-call(f32[8,1]{1,0:T(8,128)} %copy.7.heat_ref, s32[8,256]{1,0:T(8,128)} %reshape.16.place_ref, ...), custom_call_target="tpu_custom_call" | custom-call | flops 2147483648 | bytes 20971520 | tf_op jit(solution)/shard_map/band/pallas_call | solution.py:124
  26.2 2.9 %all-to-all-done.refs_0_.refs_2_ = bf16[8,2,2,64,128]{4,3,2,1,0:T(8,128)(2,1)S(1)} async-done(((bf16[8,2,2,64,128]{4,3,2,1,0:T(8,128)(2,1)}), bf16[8,2,2,64,128]{4,3,2,1,0:T(8,128)(2,1)S(1)}, u32[]{:S(2)}, u32[]{:S(2)}) %all-to-all-start) | async-done | bytes 524320 | tf_op jit(solution)/shard_map/all_to_all | solution.py:254
  29.1 0.0 copy-start.2
  29.1 0.0 collective-permute-start.1
  29.2 1.3 %collective-permute-start = (bf16[8,2,2,64,128]{4,3,2,1,0:T(8,128)(2,1)S(1)}, bf16[8,2,2,64,128]{4,3,2,1,0:T(8,128)(2,1)S(1)}, u32[]{:S(2)}, u32[]{:S(2)}) collective-permute-start(bf16[8,2,2,64,128]{4,3,2,1,0:T(8,128)(2,1)S(1)} %all-to-all-done.refs_0_.refs_2_), channel_id=1, source_target_pairs={{0,128},{1,129},{2,130},{3,131},{4,132},{5,133},{6,134},{7,135},{8... | collective-permute-start | bytes 1572872 | tf_op jit(solution)/shard_map/ppermute | solution.py:264
  30.5 4.4 %all-to-all-start.2 = ((bf16[8,2,2,64,128]{4,3,2,1,0:T(8,128)(2,1)}), bf16[8,2,2,64,128]{4,3,2,1,0:T(8,128)(2,1)S(1)}, u32[]{:S(2)}, u32[]{:S(2)}) async-start(bf16[8,2,2,64,128]{4,3,2,1,0:T(8,128)(2,1)} %get-tuple-element.32), calls=%async_computation.2 | async-start | bytes 1048576 | tf_op jit(solution)/shard_map/all_to_all | solution.py:254
  34.9 0.7 pad_add_fusion.at_ref
  35.5 0.0 collective-permute-done.1.refs_1_.refs_3_
  35.5 0.0 copy-start.5
  35.5 0.0 copy-done.2
  35.5 0.8 copy-done.5
  36.3 9.8 %own.1 = (f32[2,2048,128]{2,1,0:T(8,128)}, f32[2,2048,128]{2,1,0:T(8,128)}) custom-call(s32[3]{0:T(128)} %pad_add_fusion.at_ref, bf16[2,2048,256]{2,1,0:T(8,128)(2,1)} %get-tuple-element.22.q_ref, bf16[8,2,2,64,128]{4,3,2,1,0:T(8,128)(2,1)} %copy-done.2, bf16[8,2,2,64,128]{4,3,2,1,0:T(8,128)(2,1)} %copy-done.5, bf16[8,2,2,64,128]{4,3,2,1,0:T(8,128)(2,1)} %copy-done.2, ...), custom_call_target="tpu_custom_call" | custom-call | flops 4294967296 | bytes 12582912 | tf_op jit(solution)/shard_map/own/pallas_call | solution.py:206
  46.1 0.0 collective-permute-done.refs_0_.refs_2_
  46.1 0.0 copy-start.4
  46.2 0.3 collective-permute-start.2
  46.5 6.6 %all-to-all-done.2.refs_0_.refs_2_ = bf16[8,2,2,64,128]{4,3,2,1,0:T(8,128)(2,1)S(1)} async-done(((bf16[8,2,2,64,128]{4,3,2,1,0:T(8,128)(2,1)}), bf16[8,2,2,64,128]{4,3,2,1,0:T(8,128)(2,1)S(1)}, u32[]{:S(2)}, u32[]{:S(2)}) %all-to-all-start.2) | async-done | bytes 524320 | tf_op jit(solution)/shard_map/all_to_all | solution.py:254
  53.0 0.0 copy-start.1
  53.0 1.3 %collective-permute-start.4 = (bf16[8,2,2,64,128]{4,3,2,1,0:T(8,128)(2,1)S(1)}, bf16[8,2,2,64,128]{4,3,2,1,0:T(8,128)(2,1)S(1)}, u32[]{:S(2)}, u32[]{:S(2)}) collective-permute-start(bf16[8,2,2,64,128]{4,3,2,1,0:T(8,128)(2,1)S(1)} %all-to-all-done.2.refs_0_.refs_2_), channel_id=1, source_target_pairs={{0,128},{1,129},{2,130},{3,131},{4,132},{5,133},{6,134},{7,135},{8... | collective-permute-start | bytes 1572872 | tf_op jit(solution)/shard_map/ppermute | solution.py:270
  54.3 0.1 collective-permute-start.3
  54.5 0.0 collective-permute-done.2.refs_1_.refs_3_
  54.5 0.0 copy-start.8
  54.5 0.0 copy-done.4
  54.5 0.9 copy-done.8
  55.3 9.2 %far.1 = bf16[8,2,256,128]{3,2,1,0:T(8,128)(2,1)} custom-call(s32[3]{0:T(128)} %pad_add_fusion.at_ref, bf16[2,2048,256]{2,1,0:T(8,128)(2,1)} %get-tuple-element.22.q_ref, bf16[8,2,2,64,128]{4,3,2,1,0:T(8,128)(2,1)} %copy-done.4, bf16[8,2,2,64,128]{4,3,2,1,0:T(8,128)(2,1)} %copy-done.8, bf16[8,2,2,64,128]{4,3,2,1,0:T(8,128)(2,1)} %copy-done.4, ...), custom_call_target="tpu_custom_call" | custom-call | flops 4294967296 | bytes 12582912 | tf_op jit(solution)/shard_map/far/pallas_call | solution.py:206
  64.5 0.0 copy-done.1
  64.5 4.3 %collective-permute-done.4.refs_4_.refs_6_ = bf16[8,2,2,64,128]{4,3,2,1,0:T(8,128)(2,1)S(1)} collective-permute-done((bf16[8,2,2,64,128]{4,3,2,1,0:T(8,128)(2,1)S(1)}, bf16[8,2,2,64,128]{4,3,2,1,0:T(8,128)(2,1)S(1)}, u32[]{:S(2)}, u32[]{:S(2)}) %collective-permute-start.4) | collective-permute-done | bytes 524320 | tf_op jit(solution)/shard_map/ppermute | solution.py:270
  68.8 0.0 copy-start.6
  68.8 0.0 collective-permute-start.5
  68.8 6.0 %all-to-all-start.1 = ((bf16[8,2,256,128]{3,2,1,0:T(8,128)(2,1)}), bf16[8,2,256,128]{3,2,1,0:T(8,128)(2,1)S(1)}, u32[]{:S(2)}, u32[]{:S(2)}) async-start(bf16[8,2,256,128]{3,2,1,0:T(8,128)(2,1)} %far.1), calls=%async_computation.1 | async-start | bytes 2097152 | tf_op jit(solution)/shard_map/all_to_all | solution.py:255
  74.8 0.0 collective-permute-done.3.refs_1_.refs_3_
  74.8 0.0 copy-start.7
  74.9 0.0 collective-permute-done.5.refs_5_.refs_7_
  74.9 0.0 copy-start.9
  74.9 0.0 copy-done.6
  74.9 0.8 copy-done.7
  75.7 0.1 copy-done.9
  75.8 14.2 %own_far.1 = bf16[8,2,256,128]{3,2,1,0:T(8,128)(2,1)} custom-call(s32[3]{0:T(128)} %pad_add_fusion.at_ref, bf16[2,2048,256]{2,1,0:T(8,128)(2,1)} %get-tuple-element.30.q_ref, bf16[8,2,2,64,128]{4,3,2,1,0:T(8,128)(2,1)} %copy-done.1, bf16[8,2,2,64,128]{4,3,2,1,0:T(8,128)(2,1)} %copy-done.7, bf16[8,2,2,64,128]{4,3,2,1,0:T(8,128)(2,1)} %copy-done.1, ...), custom_call_target="tpu_custom_call" | custom-call | flops 8589934592 | bytes 12582912 | tf_op jit(solution)/shard_map/own_far/pallas_call | solution.py:206
  90.1 1.1 all-to-all-done.1.x0_ref
  91.1 0.0 copy-start
  91.1 23.6 %all_to_all.20.x1_ref = bf16[8,2,256,128]{3,2,1,0:T(8,128)(2,1)} all-to-all(bf16[8,2,256,128]{3,2,1,0:T(8,128)(2,1)} %own_far.1), channel_id=1, replica_groups=mesh['x_lo'=2,'z'=8,'core'=2,'x_hi'=2,'y'=4] {'x_hi','y'}, dimensions={0} | all-to-all | bytes 2097152 | tf_op jit(solution)/shard_map/all_to_all | solution.py:255
  114.8 0.0 copy-done
  114.8 4.0 %assemble.1 = bf16[256,32,128]{2,1,0:T(8,128)(2,1)} custom-call(bf16[8,2,256,128]{3,2,1,0:T(8,128)(2,1)} %copy-done, bf16[8,2,256,128]{3,2,1,0:T(8,128)(2,1)} %all_to_all.20.x1_ref), custom_call_target="tpu_custom_call" | custom-call | tf_op jit(solution)/shard_map/assemble/pallas_call | solution.py:234
  (1 shorter events, 0.0 us)
Async XLA Ops:
  0.0 11.6 %copy-start.10 = (f32[4]{0:T(128)S(1)}, f32[4]{0:T(128)}, u32[]{:S(2)}) copy-start(f32[4]{0:T(128)} %param.9) | copy-start | bytes 52
  0.0 12.3 %copy-start.3 = (s32[2048]{0:T(1024)S(1)}, s32[2048]{0:T(1024)}, u32[]{:S(2)}) copy-start(s32[2048]{0:T(1024)} %param.10) | copy-start | bytes 24580
  3.2 26.0 %all-to-all-start = ((bf16[8,2,2,64,128]{4,3,2,1,0:T(8,128)(2,1)}), bf16[8,2,2,64,128]{4,3,2,1,0:T(8,128)(2,1)S(1)}, u32[]{:S(2)}, u32[]{:S(2)}) async-start(bf16[8,2,2,64,128]{4,3,2,1,0:T(8,128)(2,1)} %get-tuple-element.23), calls=%async_computation | async-start | bytes 1048576 | tf_op jit(solution)/shard_map/all_to_all | solution.py:254
  29.1 6.4 %copy-start.2 = (bf16[8,2,2,64,128]{4,3,2,1,0:T(8,128)(2,1)}, bf16[8,2,2,64,128]{4,3,2,1,0:T(8,128)(2,1)S(1)}, u32[]{:S(2)}) copy-start(bf16[8,2,2,64,128]{4,3,2,1,0:T(8,128)(2,1)S(1)} %all-to-all-done.refs_0_.refs_2_) | copy-start | bytes 1572868
  29.1 6.4 %collective-permute-start.1 = (bf16[8,2,2,64,128]{4,3,2,1,0:T(8,128)(2,1)S(1)}, bf16[8,2,2,64,128]{4,3,2,1,0:T(8,128)(2,1)S(1)}, u32[]{:S(2)}, u32[]{:S(2)}) collective-permute-start(bf16[8,2,2,64,128]{4,3,2,1,0:T(8,128)(2,1)S(1)} %all-to-all-done.refs_0_.refs_2_), channel_id=1, source_target_pairs={{0,8},{8,0},{1,9},{9,1},{2,10},{10,2},{3,11},{11,3},{4,12},{12,4},... | collective-permute-start | bytes 1572872 | tf_op jit(solution)/shard_map/ppermute | solution.py:263
  29.2 17.0 %collective-permute-start = (bf16[8,2,2,64,128]{4,3,2,1,0:T(8,128)(2,1)S(1)}, bf16[8,2,2,64,128]{4,3,2,1,0:T(8,128)(2,1)S(1)}, u32[]{:S(2)}, u32[]{:S(2)}) collective-permute-start(bf16[8,2,2,64,128]{4,3,2,1,0:T(8,128)(2,1)S(1)} %all-to-all-done.refs_0_.refs_2_), channel_id=1, source_target_pairs={{0,128},{1,129},{2,130},{3,131},{4,132},{5,133},{6,134},{7,135},{8... | collective-permute-start | bytes 1572872 | tf_op jit(solution)/shard_map/ppermute | solution.py:264
  30.5 22.6 %all-to-all-start.2 = ((bf16[8,2,2,64,128]{4,3,2,1,0:T(8,128)(2,1)}), bf16[8,2,2,64,128]{4,3,2,1,0:T(8,128)(2,1)S(1)}, u32[]{:S(2)}, u32[]{:S(2)}) async-start(bf16[8,2,2,64,128]{4,3,2,1,0:T(8,128)(2,1)} %get-tuple-element.32), calls=%async_computation.2 | async-start | bytes 1048576 | tf_op jit(solution)/shard_map/all_to_all | solution.py:254
  35.5 0.8 copy-start.5
  46.1 8.3 %copy-start.4 = (bf16[8,2,2,64,128]{4,3,2,1,0:T(8,128)(2,1)}, bf16[8,2,2,64,128]{4,3,2,1,0:T(8,128)(2,1)S(1)}, u32[]{:S(2)}) copy-start(bf16[8,2,2,64,128]{4,3,2,1,0:T(8,128)(2,1)S(1)} %collective-permute-done.refs_0_.refs_2_) | copy-start | bytes 1572868
  46.2 8.3 %collective-permute-start.2 = (bf16[8,2,2,64,128]{4,3,2,1,0:T(8,128)(2,1)S(1)}, bf16[8,2,2,64,128]{4,3,2,1,0:T(8,128)(2,1)S(1)}, u32[]{:S(2)}, u32[]{:S(2)}) collective-permute-start(bf16[8,2,2,64,128]{4,3,2,1,0:T(8,128)(2,1)S(1)} %collective-permute-done.refs_0_.refs_2_), channel_id=1, source_target_pairs={{0,8},{8,0},{1,9},{9,1},{2,10},{10,2},{3,11},{11,3},{4,12},{12,4},... | collective-permute-start | bytes 1572872 | tf_op jit(solution)/shard_map/ppermute | solution.py:267
  53.0 11.5 %copy-start.1 = (bf16[8,2,2,64,128]{4,3,2,1,0:T(8,128)(2,1)}, bf16[8,2,2,64,128]{4,3,2,1,0:T(8,128)(2,1)S(1)}, u32[]{:S(2)}) copy-start(bf16[8,2,2,64,128]{4,3,2,1,0:T(8,128)(2,1)S(1)} %all-to-all-done.2.refs_0_.refs_2_) | copy-start | bytes 1572868
  53.0 15.8 %collective-permute-start.4 = (bf16[8,2,2,64,128]{4,3,2,1,0:T(8,128)(2,1)S(1)}, bf16[8,2,2,64,128]{4,3,2,1,0:T(8,128)(2,1)S(1)}, u32[]{:S(2)}, u32[]{:S(2)}) collective-permute-start(bf16[8,2,2,64,128]{4,3,2,1,0:T(8,128)(2,1)S(1)} %all-to-all-done.2.refs_0_.refs_2_), channel_id=1, source_target_pairs={{0,128},{1,129},{2,130},{3,131},{4,132},{5,133},{6,134},{7,135},{8... | collective-permute-start | bytes 1572872 | tf_op jit(solution)/shard_map/ppermute | solution.py:270
  54.3 20.5 %collective-permute-start.3 = (bf16[8,2,2,64,128]{4,3,2,1,0:T(8,128)(2,1)S(1)}, bf16[8,2,2,64,128]{4,3,2,1,0:T(8,128)(2,1)S(1)}, u32[]{:S(2)}, u32[]{:S(2)}) collective-permute-start(bf16[8,2,2,64,128]{4,3,2,1,0:T(8,128)(2,1)S(1)} %all-to-all-done.2.refs_0_.refs_2_), channel_id=1, source_target_pairs={{0,8},{8,0},{1,9},{9,1},{2,10},{10,2},{3,11},{11,3},{4,12},{12,4},... | collective-permute-start | bytes 1572872 | tf_op jit(solution)/shard_map/ppermute | solution.py:269
  54.5 0.9 copy-start.8
  68.8 6.1 %copy-start.6 = (bf16[8,2,2,64,128]{4,3,2,1,0:T(8,128)(2,1)}, bf16[8,2,2,64,128]{4,3,2,1,0:T(8,128)(2,1)S(1)}, u32[]{:S(2)}) copy-start(bf16[8,2,2,64,128]{4,3,2,1,0:T(8,128)(2,1)S(1)} %collective-permute-done.4.refs_4_.refs_6_) | copy-start | bytes 1572868
  68.8 6.1 %collective-permute-start.5 = (bf16[8,2,2,64,128]{4,3,2,1,0:T(8,128)(2,1)S(1)}, bf16[8,2,2,64,128]{4,3,2,1,0:T(8,128)(2,1)S(1)}, u32[]{:S(2)}, u32[]{:S(2)}) collective-permute-start(bf16[8,2,2,64,128]{4,3,2,1,0:T(8,128)(2,1)S(1)} %collective-permute-done.4.refs_4_.refs_6_), channel_id=1, source_target_pairs={{0,8},{8,0},{1,9},{9,1},{2,10},{10,2},{3,11},{11,3},{4,12},{12,4},... | collective-permute-start | bytes 1572872 | tf_op jit(solution)/shard_map/ppermute | solution.py:274
  68.8 22.3 %all-to-all-start.1 = ((bf16[8,2,256,128]{3,2,1,0:T(8,128)(2,1)}), bf16[8,2,256,128]{3,2,1,0:T(8,128)(2,1)S(1)}, u32[]{:S(2)}, u32[]{:S(2)}) async-start(bf16[8,2,256,128]{3,2,1,0:T(8,128)(2,1)} %far.1), calls=%async_computation.1 | async-start | bytes 2097152 | tf_op jit(solution)/shard_map/all_to_all | solution.py:255
  74.8 0.9 copy-start.7
  74.9 1.0 copy-start.9
  91.1 23.6 %copy-start = (bf16[8,2,256,128]{3,2,1,0:T(8,128)(2,1)}, bf16[8,2,256,128]{3,2,1,0:T(8,128)(2,1)S(1)}, u32[]{:S(2)}) copy-start(bf16[8,2,256,128]{3,2,1,0:T(8,128)(2,1)S(1)} %all-to-all-done.1.x0_ref) | copy-start | bytes 3145732

commit v3 on v2

--- a/solution.py
+++ b/solution.py
@@ -93,11 +93,9 @@
 
 def band_kernel(heat_ref, place_ref, q_ref, k_ref, v_ref, *refs):
     *outs, wide_ref = refs
-    j = pl.program_id(0)
-    place = place_ref[pl.ds(j, 1), :].astype(F32)
-    log_place = jnp.broadcast_to(jnp.log(1.0 + place), (8, STRIDE))
-    scale = (1.0 + heat_ref[...] * log_place) * (math.log2(math.e) / math.sqrt(DIM))
-    scale = scale.T
+    log_place = jnp.log(1.0 + place_ref[...].astype(F32))
+    rows = [1.0 + heat_ref[h] * log_place for h in range(HEADS)]
+    scale = jnp.concatenate(rows * (8 // HEADS), axis=0).T * (math.log2(math.e) / math.sqrt(DIM))
     for w, ref in enumerate((q_ref, k_ref, v_ref)):
         wide_ref[w] = ref[...].astype(F32)
     inner = [lax.broadcasted_iota(jnp.int32, (STRIDE, STRIDE), d) for d in range(2)]
@@ -117,14 +115,17 @@
 
 def band(heat, places, q, k, v):
     tokens = BLOCKS * STRIDE
-    whole = lambda *s: pl.BlockSpec(s, lambda j: (0,) * len(s))
     rows = pl.BlockSpec((STRIDE * HEADS, DIM), lambda j: (j, 0))
     out = lambda d: pl.BlockSpec((GROUP, STRIDE, d), lambda j: (0, j, 0))
     shape = lambda d, t: jax.ShapeDtypeStruct((GROUP, tokens, d), t)
     return pl.pallas_call(
         band_kernel,
         grid=(BLOCKS,),
-        in_specs=[whole(8, 1), whole(BLOCKS, STRIDE), rows, rows, rows],
+        in_specs=[
+            pl.BlockSpec(memory_space=pltpu.SMEM),
+            pl.BlockSpec((1, STRIDE), lambda j: (0, j)),
+            rows, rows, rows,
+        ],
         out_specs=[out(2 * DIM), out(DIM), out(DIM)] * 2,
         out_shape=[shape(2 * DIM, BF16), shape(DIM, F32), shape(DIM, F32)] * 2,
         scratch_shapes=[pltpu.VMEM((3, STRIDE * HEADS, DIM), F32)],
@@ -147,8 +148,8 @@
         put(j, *attend(q_ref[0, rows, :], keys, values, biases(j), m, l, acc_ref[0, rows, :]))
 
 
-def own_biases(at_ref):
-    z, core = at_ref[1], at_ref[2]
+def own_biases():
+    z, core = lax.axis_index("z"), lax.axis_index("core")
     col = lax.broadcasted_iota(jnp.int32, (1, CHIPS * COLS), 1)
     other = jnp.where(col < (z + core) * COLS, 0.0, NEG)
     return lambda j: [jnp.where(col < z * COLS + SUMM * j, 0.0, NEG), other]
@@ -158,7 +159,7 @@
     return [None, None]
 
 
-def summary_kernel(own, far, at_ref, q_ref, *refs):
+def summary_kernel(own, far, q_ref, *refs):
     kv_refs, refs = refs[: 4 * (own + far)], refs[4 * (own + far) :]
     acc_ref, ml_ref, *outs = refs
     kv = [(kv_refs[i], kv_refs[i + 2]) for s in range(own + far) for i in (4 * s, 4 * s + 1)]
@@ -172,18 +173,18 @@
         outs[0][j, 0] = (acc / l).astype(BF16)
 
     if not far:
-        attend_blocks(q_ref, kv, own_biases(at_ref), acc_ref, ml_ref, keep)
+        attend_blocks(q_ref, kv, own_biases(), acc_ref, ml_ref, keep)
         return
 
-    @pl.when(at_ref[0] == 1)
+    @pl.when(lax.axis_index("x_lo") == 1)
     def _():
-        near = own_biases(at_ref) if own else lambda j: []
+        near = own_biases() if own else lambda j: []
         attend_blocks(q_ref, kv, lambda j: near(j) + [None, None], acc_ref, ml_ref, finish)
 
-    @pl.when(at_ref[0] == 0)
+    @pl.when(lax.axis_index("x_lo") == 0)
     def _():
         if own:
-            attend_blocks(q_ref, kv[:2], own_biases(at_ref), acc_ref, ml_ref, finish)
+            attend_blocks(q_ref, kv[:2], own_biases(), acc_ref, ml_ref, finish)
         else:
             for j in range(BLOCKS):
                 rows = pl.ds(j * STRIDE, STRIDE)
@@ -191,7 +192,7 @@
                 finish(j, m, l, acc_ref[0, rows, :])
 
 
-def summaries(at, q, acc, ml, own=(), far=()):
+def summaries(q, acc, ml, own=(), far=()):
     tokens = BLOCKS * STRIDE
     kv = lambda w: pl.BlockSpec((CHIPS, 1, 1, COLS, DIM), lambda h: (0, w, h, 0, 0))
     state = lambda d: pl.BlockSpec((1, tokens, d), lambda h: (h, 0, 0))
@@ -202,12 +203,11 @@
     else:
         out_specs = [state(DIM)] * 2
         out_shape = [jax.ShapeDtypeStruct((GROUP, tokens, DIM), F32)] * 2
-    work = GROUP * tokens * 2 * CHIPS * COLS * len(sets)
+    work = GROUP * tokens * 2 * CHIPS * COLS * len(sets) // 64
     return pl.pallas_call(
         functools.partial(summary_kernel, bool(own), bool(far)),
         grid=(GROUP,),
         in_specs=[
-            pl.BlockSpec(memory_space=pltpu.SMEM),
             state(2 * DIM),
             *[kv(0), kv(0), kv(1), kv(1)] * len(sets),
             state(DIM), state(DIM),
@@ -216,10 +216,10 @@
         out_shape=out_shape,
         compiler_params=pltpu.CompilerParams(vmem_limit_bytes=60 << 20),
         cost_estimate=pl.CostEstimate(
-            flops=8 * work * DIM, bytes_accessed=12 << 20, transcendentals=work
+            flops=8 * work * DIM, bytes_accessed=work // 4, transcendentals=work
         ),
         name="_".join(n for n, s in (("own", own), ("far", far)) if s),
-    )(at, q, *[x for mine, other in sets for x in (mine, other) * 2], acc, ml)
+    )(q, *[x for mine, other in sets for x in (mine, other) * 2], acc, ml)
 
 
 def assemble_kernel(x0_ref, x1_ref, out_ref):
@@ -247,33 +247,31 @@
 
 
 def per_device(q, k, v, heat, places, shifts):
-    at = jnp.stack([lax.axis_index(a) for a in CTX]).astype(jnp.int32)
     tokens = BLOCKS * STRIDE
     swap, up = [(0, 1), (1, 0)], [(0, 1)]
     flat = lambda x: x.reshape(tokens * HEADS, DIM)
     spread = lambda x: lax.all_to_all(x, "z", 0, 0, tiled=True)
     give = lambda x: lax.all_to_all(x, HEAD, 0, 0, tiled=True)
-    heat8 = jnp.pad(heat, (0, 8 - HEADS)).reshape(8, 1)
 
     send0, send1 = gather_summaries(shifts, k, v)
     mine0 = spread(send0)
-    qs0, acc0, ml0, qs1, acc1, ml1 = band(heat8, places.reshape(BLOCKS, STRIDE), flat(q), flat(k), flat(v))
+    qs0, acc0, ml0, qs1, acc1, ml1 = band(heat, places.reshape(1, tokens), flat(q), flat(k), flat(v))
     mine0 = after(mine0, ml0)
     mine1 = spread(after(send1, mine0))
     other0 = lax.ppermute(mine0, "core", swap)
     far0 = lax.ppermute(mine0, "x_lo", up)
-    state0 = summaries(at, qs0, acc0, ml0, own=(mine0, other0))
+    state0 = summaries(qs0, acc0, ml0, own=(mine0, other0))
     far0 = after(far0, state0[1])
     far_other0 = lax.ppermute(far0, "core", swap)
-    mine1 = after(mine1, state0[1])
+    part0 = summaries(qs0, *state0, far=(far0, far_other0))
+    out0 = give(part0)
+    mine1 = after(mine1, part0)
     other1 = lax.ppermute(mine1, "core", swap)
     far1 = lax.ppermute(mine1, "x_lo", up)
-    part0 = summaries(at, qs0, *state0, far=(far0, far_other0))
-    out0 = give(part0)
-    far1 = after(far1, part0)
+    state1 = summaries(qs1, after(acc1, part0), ml1, own=(mine1, other1))
+    far1 = after(far1, state1[1])
     far_other1 = lax.ppermute(far1, "core", swap)
-    acc1 = after(acc1, part0)
-    part1 = summaries(at, qs1, acc1, ml1, own=(mine1, other1), far=(far1, far_other1))
+    part1 = summaries(qs1, *state1, far=(far1, far_other1))
     out1 = give(after(part1, out0))
     return assemble(out0, out1)
 

time: 120 us -> 117 us (0.975)
  waiting for transfers between devices: 14.8 us -> 8.72 us
  Pallas kernels: 53.7 us -> 58.4 us
    all_to_all x2, waiting for transfers between devices: 9.51 us -> 4.17 us  [per_device(): spread = lambda x: lax.all_to_all(x, 'z', 0, 0, tiled=True)]
    pallas_call x3 -> x4, Pallas kernels: 33.3 us -> 38 us  [summaries(): pl.pallas_call(functools.partial(summary_kernel, bool(own), bool(far)), g...]
    ppermute x1, waiting for transfers between devices: 4.27 us -> 0.01 us  [per_device(): far1 = lax.ppermute(mine1, 'x_lo', up)]
    ppermute x1, waiting for transfers between devices: 0.01 us -> 1.91 us  [per_device(): far_other0 = lax.ppermute(far0, 'core', swap)]
    ppermute x1, waiting for transfers between devices: 0.01 us -> 1.83 us  [per_device(): far_other1 = lax.ppermute(far1, 'core', swap)]
    reshape x3 -> x0, local copies, waits for them, and re-layouts: 1.26 us -> none  [the longest x2 0.67 us: per_device(): heat8 = jnp.pad(heat, (0, 8 - HEADS)).reshape(8, 1)]
    unnamed x22 -> x18, local copies, waits for them, and re-layouts: 2.65 us -> 3.2 us
  transfers between devices with their start and end apart: 9 -> 9, of which waited for: 4 -> 4; matrix products, arithmetic and copies ran while one was open for 2% -> 0% of each run, Pallas kernels for 39% -> 44%
where the time goes in v3:
time: 117 us; the launch traced here: 116 us
  Pallas kernels  58.4 us (50%)
  blocking collectives  24.8 us (21%)
  starting transfers between devices  21 us (18%)
  waiting for transfers between devices  8.72 us (7%)
  local copies, waits for them, and re-layouts  3.2 us (3%)
    pallas_call x4, Pallas kernels, summaries(): pl.pallas_call(functools.partial(summary_kernel, bool(own), bool(far)), g...  38 us
    all_to_all x1, blocking collectives, per_device(): give = lambda x: lax.all_to_all(x, HEAD, 0, 0, tiled=True)  24.8 us
    pallas_call x1, Pallas kernels, band(): pl.pallas_call(band_kernel, grid=(BLOCKS,), in_specs=[pl.BlockSpec(memory...  13.3 us
    all_to_all x2, starting transfers between devices, per_device(): spread = lambda x: lax.all_to_all(x, 'z', 0, 0, tiled=True)  12 us
    all_to_all x1, starting transfers between devices, per_device(): give = lambda x: lax.all_to_all(x, HEAD, 0, 0, tiled=True)  6.06 us
    all_to_all x2, waiting for transfers between devices, per_device(): spread = lambda x: lax.all_to_all(x, 'z', 0, 0, tiled=True)  4.17 us
    pallas_call x1, Pallas kernels, assemble(): pl.pallas_call(assemble_kernel, grid=(steps,), in_specs=[spec, spec], out...  4.03 us
    unnamed x18, local copies, waits for them, and re-layouts  3.2 us
  transfers between devices with their start and end apart: 9, of which 4 were waited for; matrix products, arithmetic and copies ran while one was open for 0% of the time, Pallas kernels for 44%

profile of v3, /device:TPU:2, one launch (start us, length us, event | category | flops | bytes accessed | tf_op | source)
XLA Modules:
  0.0 116.2 jit_solution(2328341435811446605)
XLA Ops:
  0.0 3.0 %gather_summaries.1 = (bf16[8,2,2,64,128]{4,3,2,1,0:T(8,128)(2,1)}, bf16[8,2,2,64,128]{4,3,2,1,0:T(8,128)(2,1)}) custom-call(s32[8,8]{1,0:T(8,128)} %shift_ref.1, bf16[2048,4,128]{2,1,0:T(4,128)(2,1)} %k_hbm.1, bf16[2048,4,128]{2,1,0:T(4,128)(2,1)} %v_hbm.1), custom_call_target="tpu_custom_call" | custom-call | tf_op jit(solution)/shard_map/gather_summaries/pallas_call | solution.py:44
  3.0 8.5 %all-to-all-start = ((bf16[8,2,2,64,128]{4,3,2,1,0:T(8,128)(2,1)}), bf16[8,2,2,64,128]{4,3,2,1,0:T(8,128)(2,1)S(1)}, u32[]{:S(2)}, u32[]{:S(2)}) async-start(bf16[8,2,2,64,128]{4,3,2,1,0:T(8,128)(2,1)} %get-tuple-element.25), calls=%async_computation | async-start | bytes 1048576 | tf_op jit(solution)/shard_map/all_to_all | solution.py:253
  11.5 13.3 %band.1 = (bf16[2,2048,256]{2,1,0:T(8,128)(2,1)}, f32[2,2048,128]{2,1,0:T(8,128)}, f32[2,2048,128]{2,1,0:T(8,128)}, bf16[2,2048,256]{2,1,0:T(8,128)(2,1)}, f32[2...) custom-call(f32[4]{0:T(128)} %heat_ref.1, s32[1,2048]{1,0:T(1,128)} %bitcast.7, bf16[8192,128]{1,0:T(8,128)(2,1)} %bitcast.6, ...), custom_call_target="tpu_custom_call" | custom-call | flops 2147483648 | bytes 20971520 | tf_op jit(solution)/shard_map/band/pallas_call | solution.py:121
  24.8 4.2 %all-to-all-done.refs_0_.refs_2_ = bf16[8,2,2,64,128]{4,3,2,1,0:T(8,128)(2,1)S(1)} async-done(((bf16[8,2,2,64,128]{4,3,2,1,0:T(8,128)(2,1)}), bf16[8,2,2,64,128]{4,3,2,1,0:T(8,128)(2,1)S(1)}, u32[]{:S(2)}, u32[]{:S(2)}) %all-to-all-start) | async-done | bytes 524320 | tf_op jit(solution)/shard_map/all_to_all | solution.py:253
  29.0 0.0 copy-start.1
  29.0 0.0 collective-permute-start.1
  29.0 1.3 %collective-permute-start = (bf16[8,2,2,64,128]{4,3,2,1,0:T(8,128)(2,1)S(1)}, bf16[8,2,2,64,128]{4,3,2,1,0:T(8,128)(2,1)S(1)}, u32[]{:S(2)}, u32[]{:S(2)}) collective-permute-start(bf16[8,2,2,64,128]{4,3,2,1,0:T(8,128)(2,1)S(1)} %all-to-all-done.refs_0_.refs_2_), channel_id=1, source_target_pairs={{0,128},{1,129},{2,130},{3,131},{4,132},{5,133},{6,134},{7,135},{8... | collective-permute-start | bytes 1572872 | tf_op jit(solution)/shard_map/ppermute | solution.py:262
  30.3 3.5 %all-to-all-start.2 = ((bf16[8,2,2,64,128]{4,3,2,1,0:T(8,128)(2,1)}), bf16[8,2,2,64,128]{4,3,2,1,0:T(8,128)(2,1)S(1)}, u32[]{:S(2)}, u32[]{:S(2)}) async-start(bf16[8,2,2,64,128]{4,3,2,1,0:T(8,128)(2,1)} %get-tuple-element.34), calls=%async_computation.2 | async-start | bytes 1048576 | tf_op jit(solution)/shard_map/all_to_all | solution.py:253
  33.8 0.0 collective-permute-done.1.refs_1_.refs_3_
  33.8 0.0 copy-start.5
  33.8 0.0 copy-done.1
  33.9 0.8 copy-done.5
  34.6 9.8 %own.2 = (f32[2,2048,128]{2,1,0:T(8,128)}, f32[2,2048,128]{2,1,0:T(8,128)}) custom-call(bf16[2,2048,256]{2,1,0:T(8,128)(2,1)} %get-tuple-element.24.q_ref, bf16[8,2,2,64,128]{4,3,2,1,0:T(8,128)(2,1)} %copy-done.1, bf16[8,2,2,64,128]{4,3,2,1,0:T(8,128)(2,1)} %copy-done.5, bf16[8,2,2,64,128]{4,3,2,1,0:T(8,128)(2,1)} %copy-done.1, ...), custom_call_target="tpu_custom_call" | custom-call | flops 67108864 | bytes 16384 | tf_op jit(solution)/shard_map/own/pallas_call | solution.py:207
  44.4 0.8 collective-permute-done.refs_0_.refs_2_
  45.2 0.0 copy-start.3
  45.2 0.0 collective-permute-start.2
  45.2 1.9 %collective-permute-done.2.refs_1_.refs_3_ = bf16[8,2,2,64,128]{4,3,2,1,0:T(8,128)(2,1)S(1)} collective-permute-done((bf16[8,2,2,64,128]{4,3,2,1,0:T(8,128)(2,1)S(1)}, bf16[8,2,2,64,128]{4,3,2,1,0:T(8,128)(2,1)S(1)}, u32[]{:S(2)}, u32[]{:S(2)}) %collective-permute-start.2) | collective-permute-done | bytes 524320 | tf_op jit(solution)/shard_map/ppermute | solution.py:265
  47.1 0.0 copy-start.7
  47.1 0.0 copy-done.3
  47.1 0.8 copy-done.7
  48.0 9.2 %far.2 = bf16[8,2,256,128]{3,2,1,0:T(8,128)(2,1)} custom-call(bf16[2,2048,256]{2,1,0:T(8,128)(2,1)} %get-tuple-element.24.q_ref, bf16[8,2,2,64,128]{4,3,2,1,0:T(8,128)(2,1)} %copy-done.3, bf16[8,2,2,64,128]{4,3,2,1,0:T(8,128)(2,1)} %copy-done.7, bf16[8,2,2,64,128]{4,3,2,1,0:T(8,128)(2,1)} %copy-done.3, bf16[8,2,2,64,128]{4,3,2,1,0:T(8,128)(2,1)} %copy-done.7, ...), custom_call_target="tpu_custom_call" | custom-call | flops 67108864 | bytes 16384 | tf_op jit(solution)/shard_map/far/pallas_call | solution.py:207
  57.2 0.0 all-to-all-done.2.refs_0_.refs_2_
  57.2 0.0 copy-start
  57.2 0.2 collective-permute-start.4
  57.4 1.3 %collective-permute-start.3 = (bf16[8,2,2,64,128]{4,3,2,1,0:T(8,128)(2,1)S(1)}, bf16[8,2,2,64,128]{4,3,2,1,0:T(8,128)(2,1)S(1)}, u32[]{:S(2)}, u32[]{:S(2)}) collective-permute-start(bf16[8,2,2,64,128]{4,3,2,1,0:T(8,128)(2,1)S(1)} %all-to-all-done.2.refs_0_.refs_2_), channel_id=1, source_target_pairs={{0,128},{1,129},{2,130},{3,131},{4,132},{5,133},{6,134},{7,135},{8... | collective-permute-start | bytes 1572872 | tf_op jit(solution)/shard_map/ppermute | solution.py:270
  58.7 6.1 %all-to-all-start.1 = ((bf16[8,2,256,128]{3,2,1,0:T(8,128)(2,1)}), bf16[8,2,256,128]{3,2,1,0:T(8,128)(2,1)S(1)}, u32[]{:S(2)}, u32[]{:S(2)}) async-start(bf16[8,2,256,128]{3,2,1,0:T(8,128)(2,1)} %far.2), calls=%async_computation.1 | async-start | bytes 2097152 | tf_op jit(solution)/shard_map/all_to_all | solution.py:254
  64.7 0.0 collective-permute-done.4.refs_1_.refs_3_
  64.8 0.0 copy-start.6
  64.8 0.0 copy-done
  64.8 0.8 copy-done.6
  65.6 9.8 %own.3 = (f32[2,2048,128]{2,1,0:T(8,128)}, f32[2,2048,128]{2,1,0:T(8,128)}) custom-call(bf16[2,2048,256]{2,1,0:T(8,128)(2,1)} %get-tuple-element.32.q_ref, bf16[8,2,2,64,128]{4,3,2,1,0:T(8,128)(2,1)} %copy-done, bf16[8,2,2,64,128]{4,3,2,1,0:T(8,128)(2,1)} %copy-done.6, bf16[8,2,2,64,128]{4,3,2,1,0:T(8,128)(2,1)} %copy-done, ...), custom_call_target="tpu_custom_call" | custom-call | flops 67108864 | bytes 16384 | tf_op jit(solution)/shard_map/own/pallas_call | solution.py:207
  75.4 0.0 collective-permute-done.3.refs_0_.refs_2_
  75.4 0.0 copy-start.4
  75.4 0.2 collective-permute-start.5
  75.6 1.8 %collective-permute-done.5.refs_1_.refs_3_ = bf16[8,2,2,64,128]{4,3,2,1,0:T(8,128)(2,1)S(1)} collective-permute-done((bf16[8,2,2,64,128]{4,3,2,1,0:T(8,128)(2,1)S(1)}, bf16[8,2,2,64,128]{4,3,2,1,0:T(8,128)(2,1)S(1)}, u32[]{:S(2)}, u32[]{:S(2)}) %collective-permute-start.5) | collective-permute-done | bytes 524320 | tf_op jit(solution)/shard_map/ppermute | solution.py:273
  77.4 0.0 copy-start.8
  77.4 0.0 copy-done.4
  77.4 0.8 copy-done.8
  78.2 9.2 %far.3 = bf16[8,2,256,128]{3,2,1,0:T(8,128)(2,1)} custom-call(bf16[2,2048,256]{2,1,0:T(8,128)(2,1)} %get-tuple-element.32.q_ref, bf16[8,2,2,64,128]{4,3,2,1,0:T(8,128)(2,1)} %copy-done.4, bf16[8,2,2,64,128]{4,3,2,1,0:T(8,128)(2,1)} %copy-done.8, bf16[8,2,2,64,128]{4,3,2,1,0:T(8,128)(2,1)} %copy-done.4, bf16[8,2,2,64,128]{4,3,2,1,0:T(8,128)(2,1)} %copy-done.8, ...), custom_call_target="tpu_custom_call" | custom-call | flops 67108864 | bytes 16384 | tf_op jit(solution)/shard_map/far/pallas_call | solution.py:207
  87.4 0.0 all-to-all-done.1.x0_ref
  87.4 0.0 copy-start.2
  87.4 24.8 %all_to_all.20.x1_ref = bf16[8,2,256,128]{3,2,1,0:T(8,128)(2,1)} all-to-all(bf16[8,2,256,128]{3,2,1,0:T(8,128)(2,1)} %far.3), channel_id=1, replica_groups=mesh['x_lo'=2,'z'=8,'core'=2,'x_hi'=2,'y'=4] {'x_hi','y'}, dimensions={0} | all-to-all | bytes 2097152 | tf_op jit(solution)/shard_map/all_to_all | solution.py:254
  112.2 0.0 copy-done.2
  112.2 4.0 %assemble.1 = bf16[256,32,128]{2,1,0:T(8,128)(2,1)} custom-call(bf16[8,2,256,128]{3,2,1,0:T(8,128)(2,1)} %copy-done.2, bf16[8,2,256,128]{3,2,1,0:T(8,128)(2,1)} %all_to_all.20.x1_ref), custom_call_target="tpu_custom_call" | custom-call | tf_op jit(solution)/shard_map/assemble/pallas_call | solution.py:234
Async XLA Ops:
  3.0 26.0 %all-to-all-start = ((bf16[8,2,2,64,128]{4,3,2,1,0:T(8,128)(2,1)}), bf16[8,2,2,64,128]{4,3,2,1,0:T(8,128)(2,1)S(1)}, u32[]{:S(2)}, u32[]{:S(2)}) async-start(bf16[8,2,2,64,128]{4,3,2,1,0:T(8,128)(2,1)} %get-tuple-element.25), calls=%async_computation | async-start | bytes 1048576 | tf_op jit(solution)/shard_map/all_to_all | solution.py:253
  29.0 4.8 %copy-start.1 = (bf16[8,2,2,64,128]{4,3,2,1,0:T(8,128)(2,1)}, bf16[8,2,2,64,128]{4,3,2,1,0:T(8,128)(2,1)S(1)}, u32[]{:S(2)}) copy-start(bf16[8,2,2,64,128]{4,3,2,1,0:T(8,128)(2,1)S(1)} %all-to-all-done.refs_0_.refs_2_) | copy-start | bytes 1572868
  29.0 4.8 %collective-permute-start.1 = (bf16[8,2,2,64,128]{4,3,2,1,0:T(8,128)(2,1)S(1)}, bf16[8,2,2,64,128]{4,3,2,1,0:T(8,128)(2,1)S(1)}, u32[]{:S(2)}, u32[]{:S(2)}) collective-permute-start(bf16[8,2,2,64,128]{4,3,2,1,0:T(8,128)(2,1)S(1)} %all-to-all-done.refs_0_.refs_2_), channel_id=1, source_target_pairs={{0,8},{8,0},{1,9},{9,1},{2,10},{10,2},{3,11},{11,3},{4,12},{12,4},... | collective-permute-start | bytes 1572872 | tf_op jit(solution)/shard_map/ppermute | solution.py:261
  29.0 16.2 %collective-permute-start = (bf16[8,2,2,64,128]{4,3,2,1,0:T(8,128)(2,1)S(1)}, bf16[8,2,2,64,128]{4,3,2,1,0:T(8,128)(2,1)S(1)}, u32[]{:S(2)}, u32[]{:S(2)}) collective-permute-start(bf16[8,2,2,64,128]{4,3,2,1,0:T(8,128)(2,1)S(1)} %all-to-all-done.refs_0_.refs_2_), channel_id=1, source_target_pairs={{0,128},{1,129},{2,130},{3,131},{4,132},{5,133},{6,134},{7,135},{8... | collective-permute-start | bytes 1572872 | tf_op jit(solution)/shard_map/ppermute | solution.py:262
  30.3 26.9 %all-to-all-start.2 = ((bf16[8,2,2,64,128]{4,3,2,1,0:T(8,128)(2,1)}), bf16[8,2,2,64,128]{4,3,2,1,0:T(8,128)(2,1)S(1)}, u32[]{:S(2)}, u32[]{:S(2)}) async-start(bf16[8,2,2,64,128]{4,3,2,1,0:T(8,128)(2,1)} %get-tuple-element.34), calls=%async_computation.2 | async-start | bytes 1048576 | tf_op jit(solution)/shard_map/all_to_all | solution.py:253
  33.8 0.8 copy-start.5
  45.2 1.9 %copy-start.3 = (bf16[8,2,2,64,128]{4,3,2,1,0:T(8,128)(2,1)}, bf16[8,2,2,64,128]{4,3,2,1,0:T(8,128)(2,1)S(1)}, u32[]{:S(2)}) copy-start(bf16[8,2,2,64,128]{4,3,2,1,0:T(8,128)(2,1)S(1)} %collective-permute-done.refs_0_.refs_2_) | copy-start | bytes 1572868
  45.2 1.9 %collective-permute-start.2 = (bf16[8,2,2,64,128]{4,3,2,1,0:T(8,128)(2,1)S(1)}, bf16[8,2,2,64,128]{4,3,2,1,0:T(8,128)(2,1)S(1)}, u32[]{:S(2)}, u32[]{:S(2)}) collective-permute-start(bf16[8,2,2,64,128]{4,3,2,1,0:T(8,128)(2,1)S(1)} %collective-permute-done.refs_0_.refs_2_), channel_id=1, source_target_pairs={{0,8},{8,0},{1,9},{9,1},{2,10},{10,2},{3,11},{11,3},{4,12},{12,4},... | collective-permute-start | bytes 1572872 | tf_op jit(solution)/shard_map/ppermute | solution.py:265
  47.1 0.8 copy-start.7
  57.2 7.6 %copy-start = (bf16[8,2,2,64,128]{4,3,2,1,0:T(8,128)(2,1)}, bf16[8,2,2,64,128]{4,3,2,1,0:T(8,128)(2,1)S(1)}, u32[]{:S(2)}) copy-start(bf16[8,2,2,64,128]{4,3,2,1,0:T(8,128)(2,1)S(1)} %all-to-all-done.2.refs_0_.refs_2_) | copy-start | bytes 1572868
  57.2 7.6 %collective-permute-start.4 = (bf16[8,2,2,64,128]{4,3,2,1,0:T(8,128)(2,1)S(1)}, bf16[8,2,2,64,128]{4,3,2,1,0:T(8,128)(2,1)S(1)}, u32[]{:S(2)}, u32[]{:S(2)}) collective-permute-start(bf16[8,2,2,64,128]{4,3,2,1,0:T(8,128)(2,1)S(1)} %all-to-all-done.2.refs_0_.refs_2_), channel_id=1, source_target_pairs={{0,8},{8,0},{1,9},{9,1},{2,10},{10,2},{3,11},{11,3},{4,12},{12,4},... | collective-permute-start | bytes 1572872 | tf_op jit(solution)/shard_map/ppermute | solution.py:269
  57.4 18.0 %collective-permute-start.3 = (bf16[8,2,2,64,128]{4,3,2,1,0:T(8,128)(2,1)S(1)}, bf16[8,2,2,64,128]{4,3,2,1,0:T(8,128)(2,1)S(1)}, u32[]{:S(2)}, u32[]{:S(2)}) collective-permute-start(bf16[8,2,2,64,128]{4,3,2,1,0:T(8,128)(2,1)S(1)} %all-to-all-done.2.refs_0_.refs_2_), channel_id=1, source_target_pairs={{0,128},{1,129},{2,130},{3,131},{4,132},{5,133},{6,134},{7,135},{8... | collective-permute-start | bytes 1572872 | tf_op jit(solution)/shard_map/ppermute | solution.py:270
  58.7 28.7 %all-to-all-start.1 = ((bf16[8,2,256,128]{3,2,1,0:T(8,128)(2,1)}), bf16[8,2,256,128]{3,2,1,0:T(8,128)(2,1)S(1)}, u32[]{:S(2)}, u32[]{:S(2)}) async-start(bf16[8,2,256,128]{3,2,1,0:T(8,128)(2,1)} %far.2), calls=%async_computation.1 | async-start | bytes 2097152 | tf_op jit(solution)/shard_map/all_to_all | solution.py:254
  64.8 0.8 copy-start.6
  75.4 2.0 %copy-start.4 = (bf16[8,2,2,64,128]{4,3,2,1,0:T(8,128)(2,1)}, bf16[8,2,2,64,128]{4,3,2,1,0:T(8,128)(2,1)S(1)}, u32[]{:S(2)}) copy-start(bf16[8,2,2,64,128]{4,3,2,1,0:T(8,128)(2,1)S(1)} %collective-permute-done.3.refs_0_.refs_2_) | copy-start | bytes 1572868
  75.4 2.0 %collective-permute-start.5 = (bf16[8,2,2,64,128]{4,3,2,1,0:T(8,128)(2,1)S(1)}, bf16[8,2,2,64,128]{4,3,2,1,0:T(8,128)(2,1)S(1)}, u32[]{:S(2)}, u32[]{:S(2)}) collective-permute-start(bf16[8,2,2,64,128]{4,3,2,1,0:T(8,128)(2,1)S(1)} %collective-permute-done.3.refs_0_.refs_2_), channel_id=1, source_target_pairs={{0,8},{8,0},{1,9},{9,1},{2,10},{10,2},{3,11},{11,3},{4,12},{12,4},... | collective-permute-start | bytes 1572872 | tf_op jit(solution)/shard_map/ppermute | solution.py:273
  77.4 0.8 copy-start.8
  87.4 24.8 %copy-start.2 = (bf16[8,2,256,128]{3,2,1,0:T(8,128)(2,1)}, bf16[8,2,256,128]{3,2,1,0:T(8,128)(2,1)S(1)}, u32[]{:S(2)}) copy-start(bf16[8,2,256,128]{3,2,1,0:T(8,128)(2,1)S(1)} %all-to-all-done.1.x0_ref) | copy-start | bytes 3145732

commit v4 on v3

--- a/solution.py
+++ b/solution.py
@@ -129,7 +129,7 @@
         out_specs=[out(2 * DIM), out(DIM), out(DIM)] * 2,
         out_shape=[shape(2 * DIM, BF16), shape(DIM, F32), shape(DIM, F32)] * 2,
         scratch_shapes=[pltpu.VMEM((3, STRIDE * HEADS, DIM), F32)],
-        compiler_params=pltpu.CompilerParams(vmem_limit_bytes=60 << 20),
+        compiler_params=pltpu.CompilerParams(vmem_limit_bytes=67_000_000),
         cost_estimate=pl.CostEstimate(
             flops=4 * HEADS * tokens * STRIDE * DIM * 2, bytes_accessed=20 << 20,
             transcendentals=HEADS * tokens * STRIDE,
@@ -138,8 +138,8 @@
     )(heat, places, q, k, v)
 
 
-def attend_blocks(q_ref, kv_refs, biases, acc_ref, ml_ref, put):
-    flat = lambda ref: ref[...].reshape(CHIPS * COLS, DIM)
+def attend_blocks(q_ref, kv_refs, biases, acc_ref, ml_ref, put, chips=CHIPS):
+    flat = lambda ref: ref[0:chips].reshape(chips * COLS, DIM)
     keys = [flat(k) for k, _ in kv_refs]
     values = [flat(v) for _, v in kv_refs]
     for j in range(BLOCKS):
@@ -148,9 +148,9 @@
         put(j, *attend(q_ref[0, rows, :], keys, values, biases(j), m, l, acc_ref[0, rows, :]))
 
 
-def own_biases():
+def own_biases(chips=CHIPS):
     z, core = lax.axis_index("z"), lax.axis_index("core")
-    col = lax.broadcasted_iota(jnp.int32, (1, CHIPS * COLS), 1)
+    col = lax.broadcasted_iota(jnp.int32, (1, chips * COLS), 1)
     other = jnp.where(col < (z + core) * COLS, 0.0, NEG)
     return lambda j: [jnp.where(col < z * COLS + SUMM * j, 0.0, NEG), other]
 
@@ -173,7 +173,13 @@
         outs[0][j, 0] = (acc / l).astype(BF16)
 
     if not far:
-        attend_blocks(q_ref, kv, own_biases(), acc_ref, ml_ref, keep)
+        low = lax.axis_index("z") < CHIPS // 2
+        for chips, here in ((CHIPS // 2, low), (CHIPS, jnp.logical_not(low))):
+
+            @pl.when(here)
+            def _(chips=chips):
+                attend_blocks(q_ref, kv, own_biases(chips), acc_ref, ml_ref, keep, chips)
+
         return
 
     @pl.when(lax.axis_index("x_lo") == 1)
@@ -214,7 +220,7 @@
         ],
         out_specs=out_specs,
         out_shape=out_shape,
-        compiler_params=pltpu.CompilerParams(vmem_limit_bytes=60 << 20),
+        compiler_params=pltpu.CompilerParams(vmem_limit_bytes=67_000_000),
         cost_estimate=pl.CostEstimate(
             flops=8 * work * DIM, bytes_accessed=work // 4, transcendentals=work
         ),
@@ -237,7 +243,7 @@
         in_specs=[spec, spec],
         out_specs=pl.BlockSpec((count, total, DIM), lambda t: (t, 0, 0)),
         out_shape=jax.ShapeDtypeStruct((STRIDE, total, DIM), BF16),
-        compiler_params=pltpu.CompilerParams(vmem_limit_bytes=60 << 20),
+        compiler_params=pltpu.CompilerParams(vmem_limit_bytes=67_000_000),
         name="assemble",
     )(x0, x1)
 

time: 117 us -> 116 us (level)
  local copies, waits for them, and re-layouts: 3.2 us -> 0 us
    unnamed x18 -> x0, local copies, waits for them, and re-layouts: 3.2 us -> none
  transfers between devices with their start and end apart: 9 -> 9, of which waited for: 4 -> 4; matrix products, arithmetic and copies ran while one was open for 0% -> 0% of each run, Pallas kernels for 44% -> 45%
where the time goes in v4:
time: 116 us; the launch traced here: 115 us
  Pallas kernels  58.9 us (51%)
  blocking collectives  24.8 us (21%)
  starting transfers between devices  21.9 us (19%)
  waiting for transfers between devices  9.77 us (8%)
    pallas_call x4, Pallas kernels, summaries(): pl.pallas_call(functools.partial(summary_kernel, bool(own), bool(far)), g...  38.5 us
    all_to_all x1, blocking collectives, per_device(): give = lambda x: lax.all_to_all(x, HEAD, 0, 0, tiled=True)  24.8 us
    pallas_call x1, Pallas kernels, band(): pl.pallas_call(band_kernel, grid=(BLOCKS,), in_specs=[pl.BlockSpec(memory...  13.3 us
    all_to_all x2, starting transfers between devices, per_device(): spread = lambda x: lax.all_to_all(x, 'z', 0, 0, tiled=True)  12.6 us
    all_to_all x1, starting transfers between devices, per_device(): give = lambda x: lax.all_to_all(x, HEAD, 0, 0, tiled=True)  6.06 us
    all_to_all x2, waiting for transfers between devices, per_device(): spread = lambda x: lax.all_to_all(x, 'z', 0, 0, tiled=True)  4.3 us
    pallas_call x1, Pallas kernels, assemble(): pl.pallas_call(assemble_kernel, grid=(steps,), in_specs=[spec, spec], out...  4.03 us
    pallas_call x1, Pallas kernels, gather_summaries(): pl.pallas_call(gather_kernel, in_specs=[pl.BlockSpec(memory_space=pltpu.S...  3.06 us
  transfers between devices with their start and end apart: 9, of which 4 were waited for; matrix products, arithmetic and copies ran while one was open for 0% of the time, Pallas kernels for 45%

profile of v4, /device:TPU:2, one launch (start us, length us, event | category | flops | bytes accessed | tf_op | source)
XLA Modules:
  0.0 115.3 jit_solution(8443401631535251651)
XLA Ops:
  0.0 3.1 %gather_summaries.1 = (bf16[8,2,2,64,128]{4,3,2,1,0:T(8,128)(2,1)}, bf16[8,2,2,64,128]{4,3,2,1,0:T(8,128)(2,1)}) custom-call(s32[8,8]{1,0:T(8,128)} %shift_ref.1, bf16[2048,4,128]{2,1,0:T(4,128)(2,1)} %k_hbm.1, bf16[2048,4,128]{2,1,0:T(4,128)(2,1)} %v_hbm.1), custom_call_target="tpu_custom_call" | custom-call | tf_op jit(solution)/shard_map/gather_summaries/pallas_call | solution.py:44
  3.1 8.5 %all-to-all-start = ((bf16[8,2,2,64,128]{4,3,2,1,0:T(8,128)(2,1)}), bf16[8,2,2,64,128]{4,3,2,1,0:T(8,128)(2,1)}, u32[]{:S(2)}, u32[]{:S(2)}) async-start(bf16[8,2,2,64,128]{4,3,2,1,0:T(8,128)(2,1)} %get-tuple-element.25), calls=%async_computation | async-start | bytes 1048576 | tf_op jit(solution)/shard_map/all_to_all | solution.py:259
  11.5 13.3 %band.1 = (bf16[2,2048,256]{2,1,0:T(8,128)(2,1)}, f32[2,2048,128]{2,1,0:T(8,128)}, f32[2,2048,128]{2,1,0:T(8,128)}, bf16[2,2048,256]{2,1,0:T(8,128)(2,1)}, f32[2...) custom-call(f32[4]{0:T(128)} %heat_ref.1, s32[1,2048]{1,0:T(1,128)} %bitcast.7, bf16[8192,128]{1,0:T(8,128)(2,1)} %bitcast.6, ...), custom_call_target="tpu_custom_call" | custom-call | flops 2147483648 | bytes 20971520 | tf_op jit(solution)/shard_map/band/pallas_call | solution.py:121
  24.9 4.3 %all-to-all-done.refs_0_.refs_2_ = bf16[8,2,2,64,128]{4,3,2,1,0:T(8,128)(2,1)} async-done(((bf16[8,2,2,64,128]{4,3,2,1,0:T(8,128)(2,1)}), bf16[8,2,2,64,128]{4,3,2,1,0:T(8,128)(2,1)}, u32[]{:S(2)}, u32[]{:S(2)}) %all-to-all-start) | async-done | bytes 524320 | tf_op jit(solution)/shard_map/all_to_all | solution.py:259
  29.1 0.0 collective-permute-start.1
  29.2 1.3 %collective-permute-start = (bf16[8,2,2,64,128]{4,3,2,1,0:T(8,128)(2,1)}, bf16[8,2,2,64,128]{4,3,2,1,0:T(8,128)(2,1)}, u32[]{:S(2)}, u32[]{:S(2)}) collective-permute-start(bf16[8,2,2,64,128]{4,3,2,1,0:T(8,128)(2,1)} %all-to-all-done.refs_0_.refs_2_), channel_id=1, source_target_pairs={{0,128},{1,129},{2,130},{3,131},{4,132},{5,133},{6,134},{7,135},{8... | collective-permute-start | bytes 1572872 | tf_op jit(solution)/shard_map/ppermute | solution.py:268
  30.5 4.2 %all-to-all-start.2 = ((bf16[8,2,2,64,128]{4,3,2,1,0:T(8,128)(2,1)}), bf16[8,2,2,64,128]{4,3,2,1,0:T(8,128)(2,1)}, u32[]{:S(2)}, u32[]{:S(2)}) async-start(bf16[8,2,2,64,128]{4,3,2,1,0:T(8,128)(2,1)} %get-tuple-element.34), calls=%async_computation.2 | async-start | bytes 1048576 | tf_op jit(solution)/shard_map/all_to_all | solution.py:259
  34.6 0.0 collective-permute-done.1.refs_1_.refs_3_
  34.6 10.0 %own.2 = (f32[2,2048,128]{2,1,0:T(8,128)}, f32[2,2048,128]{2,1,0:T(8,128)}) custom-call(bf16[2,2048,256]{2,1,0:T(8,128)(2,1)} %get-tuple-element.24.q_ref, bf16[8,2,2,64,128]{4,3,2,1,0:T(8,128)(2,1)} %all-to-all-done.refs_0_.refs_2_, bf16[8,2,2,64,128]{4,3,2,1,0:T(8,128)(2,1)} %collective-permute-done.1.refs_1_.refs_3_, ...), custom_call_target="tpu_custom_call" | custom-call | flops 67108864 | bytes 16384 | tf_op jit(solution)/shard_map/own/pallas_call | solution.py:213
  44.6 1.0 collective-permute-done.refs_0_.refs_2_
  45.7 0.0 collective-permute-start.2
  45.7 2.2 %collective-permute-done.2.refs_1_.refs_3_ = bf16[8,2,2,64,128]{4,3,2,1,0:T(8,128)(2,1)} collective-permute-done((bf16[8,2,2,64,128]{4,3,2,1,0:T(8,128)(2,1)}, bf16[8,2,2,64,128]{4,3,2,1,0:T(8,128)(2,1)}, u32[]{:S(2)}, u32[]{:S(2)}) %collective-permute-start.2) | collective-permute-done | bytes 524320 | tf_op jit(solution)/shard_map/ppermute | solution.py:271
  47.9 9.2 %far.2 = bf16[8,2,256,128]{3,2,1,0:T(8,128)(2,1)} custom-call(bf16[2,2048,256]{2,1,0:T(8,128)(2,1)} %get-tuple-element.24.q_ref, bf16[8,2,2,64,128]{4,3,2,1,0:T(8,128)(2,1)} %collective-permute-done.refs_0_.refs_2_, bf16[8,2,2,64,128]{4,3,2,1,0:T(8,128)(2,1)} %collective-permute-done.2.refs_1_.refs_3_, ...), custom_call_target="tpu_custom_call" | custom-call | flops 67108864 | bytes 16384 | tf_op jit(solution)/shard_map/far/pallas_call | solution.py:213
  57.2 0.0 all-to-all-done.2.refs_0_.refs_2_
  57.2 0.2 collective-permute-start.4
  57.4 1.3 %collective-permute-start.3 = (bf16[8,2,2,64,128]{4,3,2,1,0:T(8,128)(2,1)}, bf16[8,2,2,64,128]{4,3,2,1,0:T(8,128)(2,1)}, u32[]{:S(2)}, u32[]{:S(2)}) collective-permute-start(bf16[8,2,2,64,128]{4,3,2,1,0:T(8,128)(2,1)} %all-to-all-done.2.refs_0_.refs_2_), channel_id=1, source_target_pairs={{0,128},{1,129},{2,130},{3,131},{4,132},{5,133},{6,134},{7,135},{8... | collective-permute-start | bytes 1572872 | tf_op jit(solution)/shard_map/ppermute | solution.py:276
  58.7 6.1 %all-to-all-start.1 = ((bf16[8,2,256,128]{3,2,1,0:T(8,128)(2,1)}), bf16[8,2,256,128]{3,2,1,0:T(8,128)(2,1)}, u32[]{:S(2)}, u32[]{:S(2)}) async-start(bf16[8,2,256,128]{3,2,1,0:T(8,128)(2,1)} %far.2), calls=%async_computation.1 | async-start | bytes 2097152 | tf_op jit(solution)/shard_map/all_to_all | solution.py:260
  64.7 0.0 collective-permute-done.4.refs_1_.refs_3_
  64.7 10.1 %own.3 = (f32[2,2048,128]{2,1,0:T(8,128)}, f32[2,2048,128]{2,1,0:T(8,128)}) custom-call(bf16[2,2048,256]{2,1,0:T(8,128)(2,1)} %get-tuple-element.32.q_ref, bf16[8,2,2,64,128]{4,3,2,1,0:T(8,128)(2,1)} %all-to-all-done.2.refs_0_.refs_2_, bf16[8,2,2,64,128]{4,3,2,1,0:T(8,128)(2,1)} %collective-permute-done.4.refs_1_.refs_3_, ...), custom_call_target="tpu_custom_call" | custom-call | flops 67108864 | bytes 16384 | tf_op jit(solution)/shard_map/own/pallas_call | solution.py:213
  74.8 0.0 collective-permute-done.3.refs_0_.refs_2_
  74.8 0.4 collective-permute-start.5
  75.2 2.2 %collective-permute-done.5.refs_1_.refs_3_ = bf16[8,2,2,64,128]{4,3,2,1,0:T(8,128)(2,1)} collective-permute-done((bf16[8,2,2,64,128]{4,3,2,1,0:T(8,128)(2,1)}, bf16[8,2,2,64,128]{4,3,2,1,0:T(8,128)(2,1)}, u32[]{:S(2)}, u32[]{:S(2)}) %collective-permute-start.5) | collective-permute-done | bytes 524320 | tf_op jit(solution)/shard_map/ppermute | solution.py:279
  77.3 9.2 %far.3 = bf16[8,2,256,128]{3,2,1,0:T(8,128)(2,1)} custom-call(bf16[2,2048,256]{2,1,0:T(8,128)(2,1)} %get-tuple-element.32.q_ref, bf16[8,2,2,64,128]{4,3,2,1,0:T(8,128)(2,1)} %collective-permute-done.3.refs_0_.refs_2_, bf16[8,2,2,64,128]{4,3,2,1,0:T(8,128)(2,1)} %collective-permute-done.5.refs_1_.refs_3_, ...), custom_call_target="tpu_custom_call" | custom-call | flops 67108864 | bytes 16384 | tf_op jit(solution)/shard_map/far/pallas_call | solution.py:213
  86.5 0.0 all-to-all-done.1.x0_ref
  86.5 24.8 %all_to_all.20.x1_ref = bf16[8,2,256,128]{3,2,1,0:T(8,128)(2,1)} all-to-all(bf16[8,2,256,128]{3,2,1,0:T(8,128)(2,1)} %far.3), channel_id=1, replica_groups=mesh['x_lo'=2,'z'=8,'core'=2,'x_hi'=2,'y'=4] {'x_hi','y'}, dimensions={0} | all-to-all | bytes 2097152 | tf_op jit(solution)/shard_map/all_to_all | solution.py:260
  111.3 4.0 %assemble.1 = bf16[256,32,128]{2,1,0:T(8,128)(2,1)} custom-call(bf16[8,2,256,128]{3,2,1,0:T(8,128)(2,1)} %all-to-all-done.1.x0_ref, bf16[8,2,256,128]{3,2,1,0:T(8,128)(2,1)} %all_to_all.20.x1_ref), custom_call_target="tpu_custom_call" | custom-call | tf_op jit(solution)/shard_map/assemble/pallas_call | solution.py:240
Async XLA Ops:
  3.1 26.1 %all-to-all-start = ((bf16[8,2,2,64,128]{4,3,2,1,0:T(8,128)(2,1)}), bf16[8,2,2,64,128]{4,3,2,1,0:T(8,128)(2,1)}, u32[]{:S(2)}, u32[]{:S(2)}) async-start(bf16[8,2,2,64,128]{4,3,2,1,0:T(8,128)(2,1)} %get-tuple-element.25), calls=%async_computation | async-start | bytes 1048576 | tf_op jit(solution)/shard_map/all_to_all | solution.py:259
  29.1 5.5 %collective-permute-start.1 = (bf16[8,2,2,64,128]{4,3,2,1,0:T(8,128)(2,1)}, bf16[8,2,2,64,128]{4,3,2,1,0:T(8,128)(2,1)}, u32[]{:S(2)}, u32[]{:S(2)}) collective-permute-start(bf16[8,2,2,64,128]{4,3,2,1,0:T(8,128)(2,1)} %all-to-all-done.refs_0_.refs_2_), channel_id=1, source_target_pairs={{0,8},{8,0},{1,9},{9,1},{2,10},{10,2},{3,11},{11,3},{4,12},{12,4},... | collective-permute-start | bytes 1572872 | tf_op jit(solution)/shard_map/ppermute | solution.py:267
  29.2 16.5 %collective-permute-start = (bf16[8,2,2,64,128]{4,3,2,1,0:T(8,128)(2,1)}, bf16[8,2,2,64,128]{4,3,2,1,0:T(8,128)(2,1)}, u32[]{:S(2)}, u32[]{:S(2)}) collective-permute-start(bf16[8,2,2,64,128]{4,3,2,1,0:T(8,128)(2,1)} %all-to-all-done.refs_0_.refs_2_), channel_id=1, source_target_pairs={{0,128},{1,129},{2,130},{3,131},{4,132},{5,133},{6,134},{7,135},{8... | collective-permute-start | bytes 1572872 | tf_op jit(solution)/shard_map/ppermute | solution.py:268
  30.5 26.7 %all-to-all-start.2 = ((bf16[8,2,2,64,128]{4,3,2,1,0:T(8,128)(2,1)}), bf16[8,2,2,64,128]{4,3,2,1,0:T(8,128)(2,1)}, u32[]{:S(2)}, u32[]{:S(2)}) async-start(bf16[8,2,2,64,128]{4,3,2,1,0:T(8,128)(2,1)} %get-tuple-element.34), calls=%async_computation.2 | async-start | bytes 1048576 | tf_op jit(solution)/shard_map/all_to_all | solution.py:259
  45.7 2.3 %collective-permute-start.2 = (bf16[8,2,2,64,128]{4,3,2,1,0:T(8,128)(2,1)}, bf16[8,2,2,64,128]{4,3,2,1,0:T(8,128)(2,1)}, u32[]{:S(2)}, u32[]{:S(2)}) collective-permute-start(bf16[8,2,2,64,128]{4,3,2,1,0:T(8,128)(2,1)} %collective-permute-done.refs_0_.refs_2_), channel_id=1, source_target_pairs={{0,8},{8,0},{1,9},{9,1},{2,10},{10,2},{3,11},{11,3},{4,12},{12,4},... | collective-permute-start | bytes 1572872 | tf_op jit(solution)/shard_map/ppermute | solution.py:271
  57.2 7.6 %collective-permute-start.4 = (bf16[8,2,2,64,128]{4,3,2,1,0:T(8,128)(2,1)}, bf16[8,2,2,64,128]{4,3,2,1,0:T(8,128)(2,1)}, u32[]{:S(2)}, u32[]{:S(2)}) collective-permute-start(bf16[8,2,2,64,128]{4,3,2,1,0:T(8,128)(2,1)} %all-to-all-done.2.refs_0_.refs_2_), channel_id=1, source_target_pairs={{0,8},{8,0},{1,9},{9,1},{2,10},{10,2},{3,11},{11,3},{4,12},{12,4},... | collective-permute-start | bytes 1572872 | tf_op jit(solution)/shard_map/ppermute | solution.py:275
  57.4 17.4 %collective-permute-start.3 = (bf16[8,2,2,64,128]{4,3,2,1,0:T(8,128)(2,1)}, bf16[8,2,2,64,128]{4,3,2,1,0:T(8,128)(2,1)}, u32[]{:S(2)}, u32[]{:S(2)}) collective-permute-start(bf16[8,2,2,64,128]{4,3,2,1,0:T(8,128)(2,1)} %all-to-all-done.2.refs_0_.refs_2_), channel_id=1, source_target_pairs={{0,128},{1,129},{2,130},{3,131},{4,132},{5,133},{6,134},{7,135},{8... | collective-permute-start | bytes 1572872 | tf_op jit(solution)/shard_map/ppermute | solution.py:276
  58.7 27.9 %all-to-all-start.1 = ((bf16[8,2,256,128]{3,2,1,0:T(8,128)(2,1)}), bf16[8,2,256,128]{3,2,1,0:T(8,128)(2,1)}, u32[]{:S(2)}, u32[]{:S(2)}) async-start(bf16[8,2,256,128]{3,2,1,0:T(8,128)(2,1)} %far.2), calls=%async_computation.1 | async-start | bytes 2097152 | tf_op jit(solution)/shard_map/all_to_all | solution.py:260
  74.8 2.6 %collective-permute-start.5 = (bf16[8,2,2,64,128]{4,3,2,1,0:T(8,128)(2,1)}, bf16[8,2,2,64,128]{4,3,2,1,0:T(8,128)(2,1)}, u32[]{:S(2)}, u32[]{:S(2)}) collective-permute-start(bf16[8,2,2,64,128]{4,3,2,1,0:T(8,128)(2,1)} %collective-permute-done.3.refs_0_.refs_2_), channel_id=1, source_target_pairs={{0,8},{8,0},{1,9},{9,1},{2,10},{10,2},{3,11},{11,3},{4,12},{12,4},... | collective-permute-start | bytes 1572872 | tf_op jit(solution)/shard_map/ppermute | solution.py:279

commit v5 on v4

--- a/solution.py
+++ b/solution.py
@@ -58,13 +58,17 @@
     )(digest_shifts, keys, values)
 
 
-def attend(q, keys, values, biases, m, l, acc):
+def score(q, keys, biases):
     scores = []
     for k, bias in zip(keys, biases):
         s = lax.dot_general(
             q, jnp.concatenate([k, k], axis=1), TRANS_B, preferred_element_type=F32
         )
         scores.append(s if bias is None else s + bias)
+    return scores
+
+
+def attend(scores, values, m, l, acc):
     top = m
     for s in scores:
         peak = s.max(axis=1, keepdims=True)
@@ -100,15 +104,19 @@
         wide_ref[w] = ref[...].astype(F32)
     inner = [lax.broadcasted_iota(jnp.int32, (STRIDE, STRIDE), d) for d in range(2)]
     bias = jnp.where(inner[0] >= inner[1], 0.0, NEG)
+    queries, scores, values = [], [], []
     for h in range(HEADS):
         q, k, v = (wide_ref[w, pl.ds(h, STRIDE, stride=HEADS), :] for w in range(3))
         q = q * scale[:, h : h + 1]
         high = q.astype(BF16)
         low = (q - high.astype(F32)).astype(BF16)
-        q = jnp.concatenate([high, low], axis=1)
-        m, l, acc = attend(q, (k.astype(BF16),), (v.astype(BF16),), (bias,), None, None, None)
+        queries.append(jnp.concatenate([high, low], axis=1))
+        scores.append(score(queries[h], (k.astype(BF16),), (bias,)))
+        values.append(v.astype(BF16))
+    for h in range(HEADS):
+        m, l, acc = attend(scores[h], (values[h],), None, None, None)
         qs_ref, acc_ref, ml_ref = outs[3 * (h // GROUP) :][:3]
-        qs_ref[h % GROUP] = q
+        qs_ref[h % GROUP] = queries[h]
         acc_ref[h % GROUP] = acc
         ml_ref[h % GROUP] = pack_stats(m, l)
 
@@ -142,10 +150,13 @@
     flat = lambda ref: ref[0:chips].reshape(chips * COLS, DIM)
     keys = [flat(k) for k, _ in kv_refs]
     values = [flat(v) for _, v in kv_refs]
+    scores = lambda j: score(q_ref[0, pl.ds(j * STRIDE, STRIDE), :], keys, biases(j))
+    ahead = scores(0)
     for j in range(BLOCKS):
+        now, ahead = ahead, scores(j + 1) if j + 1 < BLOCKS else None
         rows = pl.ds(j * STRIDE, STRIDE)
         m, l = unpack_stats(ml_ref[0, rows, :])
-        put(j, *attend(q_ref[0, rows, :], keys, values, biases(j), m, l, acc_ref[0, rows, :]))
+        put(j, *attend(now, values, m, l, acc_ref[0, rows, :]))
 
 
 def own_biases(chips=CHIPS):

time: 116 us -> 113 us (0.974)
  Pallas kernels: 58.9 us -> 52.6 us
  waiting for transfers between devices: 9.77 us -> 14.9 us
  blocking collectives: 24.8 us -> 23.6 us
    pallas_call x4, Pallas kernels: 38.5 us -> 33.8 us  [summaries(): pl.pallas_call(functools.partial(summary_kernel, bool(own), bool(far)), g...]
    ppermute x1, waiting for transfers between devices: 1.04 us -> 2.99 us  [per_device(): far0 = lax.ppermute(mine0, 'x_lo', up)]
    all_to_all x2, waiting for transfers between devices: 4.3 us -> 5.9 us  [per_device(): spread = lambda x: lax.all_to_all(x, 'z', 0, 0, tiled=True)]
    pallas_call x1, Pallas kernels: 13.3 us -> 11.7 us  [band(): pl.pallas_call(band_kernel, grid=(BLOCKS,), in_specs=[pl.BlockSpec(memory...]
    ppermute x1, waiting for transfers between devices: 0.01 us -> 1.5 us  [per_device(): far1 = lax.ppermute(mine1, 'x_lo', up)]
    all_to_all x1, blocking collectives: 24.8 us -> 23.6 us  [per_device(): give = lambda x: lax.all_to_all(x, HEAD, 0, 0, tiled=True)]
  transfers between devices with their start and end apart: 9 -> 9, of which waited for: 4 -> 5; matrix products, arithmetic and copies ran while one was open for 0% -> 0% of each run, Pallas kernels for 45% -> 40%
where the time goes in v5:
time: 113 us
  Pallas kernels  52.6 us (47%)
  blocking collectives  23.6 us (21%)
  starting transfers between devices  21.5 us (19%)
  waiting for transfers between devices  14.9 us (13%)
    pallas_call x4, Pallas kernels, summaries(): pl.pallas_call(functools.partial(summary_kernel, bool(own), bool(far)), g...  33.8 us
    all_to_all x1, blocking collectives, per_device(): give = lambda x: lax.all_to_all(x, HEAD, 0, 0, tiled=True)  23.6 us
    all_to_all x2, starting transfers between devices, per_device(): spread = lambda x: lax.all_to_all(x, 'z', 0, 0, tiled=True)  12.6 us
    pallas_call x1, Pallas kernels, band(): pl.pallas_call(band_kernel, grid=(BLOCKS,), in_specs=[pl.BlockSpec(memory...  11.7 us
    all_to_all x1, starting transfers between devices, per_device(): give = lambda x: lax.all_to_all(x, HEAD, 0, 0, tiled=True)  6.06 us
    all_to_all x2, waiting for transfers between devices, per_device(): spread = lambda x: lax.all_to_all(x, 'z', 0, 0, tiled=True)  5.9 us
    pallas_call x1, Pallas kernels, assemble(): pl.pallas_call(assemble_kernel, grid=(steps,), in_specs=[spec, spec], out...  4.03 us
    pallas_call x1, Pallas kernels, gather_summaries(): pl.pallas_call(gather_kernel, in_specs=[pl.BlockSpec(memory_space=pltpu.S...  3.06 us
  transfers between devices with their start and end apart: 9, of which 5 were waited for; matrix products, arithmetic and copies ran while one was open for 0% of the time, Pallas kernels for 40%

profile of v5, /device:TPU:2, one launch (start us, length us, event | category | flops | bytes accessed | tf_op | source)
XLA Modules:
  0.0 112.6 jit_solution(17983958967697583883)
XLA Ops:
  0.0 3.1 %gather_summaries.1 = (bf16[8,2,2,64,128]{4,3,2,1,0:T(8,128)(2,1)}, bf16[8,2,2,64,128]{4,3,2,1,0:T(8,128)(2,1)}) custom-call(s32[8,8]{1,0:T(8,128)} %shift_ref.1, bf16[2048,4,128]{2,1,0:T(4,128)(2,1)} %k_hbm.1, bf16[2048,4,128]{2,1,0:T(4,128)(2,1)} %v_hbm.1), custom_call_target="tpu_custom_call" | custom-call | tf_op jit(solution)/shard_map/gather_summaries/pallas_call | solution.py:44
  3.1 8.5 %all-to-all-start = ((bf16[8,2,2,64,128]{4,3,2,1,0:T(8,128)(2,1)}), bf16[8,2,2,64,128]{4,3,2,1,0:T(8,128)(2,1)}, u32[]{:S(2)}, u32[]{:S(2)}) async-start(bf16[8,2,2,64,128]{4,3,2,1,0:T(8,128)(2,1)} %get-tuple-element.25), calls=%async_computation | async-start | bytes 1048576 | tf_op jit(solution)/shard_map/all_to_all | solution.py:270
  11.5 11.7 %band.1 = (bf16[2,2048,256]{2,1,0:T(8,128)(2,1)}, f32[2,2048,128]{2,1,0:T(8,128)}, f32[2,2048,128]{2,1,0:T(8,128)}, bf16[2,2048,256]{2,1,0:T(8,128)(2,1)}, f32[2...) custom-call(f32[4]{0:T(128)} %heat_ref.1, s32[1,2048]{1,0:T(1,128)} %bitcast.7, bf16[8192,128]{1,0:T(8,128)(2,1)} %bitcast.6, ...), custom_call_target="tpu_custom_call" | custom-call | flops 2147483648 | bytes 20971520 | tf_op jit(solution)/shard_map/band/pallas_call | solution.py:129
  23.3 5.9 %all-to-all-done.refs_0_.refs_2_ = bf16[8,2,2,64,128]{4,3,2,1,0:T(8,128)(2,1)} async-done(((bf16[8,2,2,64,128]{4,3,2,1,0:T(8,128)(2,1)}), bf16[8,2,2,64,128]{4,3,2,1,0:T(8,128)(2,1)}, u32[]{:S(2)}, u32[]{:S(2)}) %all-to-all-start) | async-done | bytes 524320 | tf_op jit(solution)/shard_map/all_to_all | solution.py:270
  29.1 0.0 collective-permute-start.1
  29.2 1.3 %collective-permute-start = (bf16[8,2,2,64,128]{4,3,2,1,0:T(8,128)(2,1)}, bf16[8,2,2,64,128]{4,3,2,1,0:T(8,128)(2,1)}, u32[]{:S(2)}, u32[]{:S(2)}) collective-permute-start(bf16[8,2,2,64,128]{4,3,2,1,0:T(8,128)(2,1)} %all-to-all-done.refs_0_.refs_2_), channel_id=1, source_target_pairs={{0,128},{1,129},{2,130},{3,131},{4,132},{5,133},{6,134},{7,135},{8... | collective-permute-start | bytes 1572872 | tf_op jit(solution)/shard_map/ppermute | solution.py:279
  30.5 4.2 %all-to-all-start.2 = ((bf16[8,2,2,64,128]{4,3,2,1,0:T(8,128)(2,1)}), bf16[8,2,2,64,128]{4,3,2,1,0:T(8,128)(2,1)}, u32[]{:S(2)}, u32[]{:S(2)}) async-start(bf16[8,2,2,64,128]{4,3,2,1,0:T(8,128)(2,1)} %get-tuple-element.34), calls=%async_computation.2 | async-start | bytes 1048576 | tf_op jit(solution)/shard_map/all_to_all | solution.py:270
  34.6 0.0 collective-permute-done.1.refs_1_.refs_3_
  34.6 8.1 %own.2 = (f32[2,2048,128]{2,1,0:T(8,128)}, f32[2,2048,128]{2,1,0:T(8,128)}) custom-call(bf16[2,2048,256]{2,1,0:T(8,128)(2,1)} %get-tuple-element.24.q_ref, bf16[8,2,2,64,128]{4,3,2,1,0:T(8,128)(2,1)} %all-to-all-done.refs_0_.refs_2_, bf16[8,2,2,64,128]{4,3,2,1,0:T(8,128)(2,1)} %collective-permute-done.1.refs_1_.refs_3_, ...), custom_call_target="tpu_custom_call" | custom-call | flops 67108864 | bytes 16384 | tf_op jit(solution)/shard_map/own/pallas_call | solution.py:224
  42.7 3.0 %collective-permute-done.refs_0_.refs_2_ = bf16[8,2,2,64,128]{4,3,2,1,0:T(8,128)(2,1)} collective-permute-done((bf16[8,2,2,64,128]{4,3,2,1,0:T(8,128)(2,1)}, bf16[8,2,2,64,128]{4,3,2,1,0:T(8,128)(2,1)}, u32[]{:S(2)}, u32[]{:S(2)}) %collective-permute-start) | collective-permute-done | bytes 524320 | tf_op jit(solution)/shard_map/ppermute | solution.py:279
  45.7 0.0 collective-permute-start.2
  45.7 2.2 %collective-permute-done.2.refs_1_.refs_3_ = bf16[8,2,2,64,128]{4,3,2,1,0:T(8,128)(2,1)} collective-permute-done((bf16[8,2,2,64,128]{4,3,2,1,0:T(8,128)(2,1)}, bf16[8,2,2,64,128]{4,3,2,1,0:T(8,128)(2,1)}, u32[]{:S(2)}, u32[]{:S(2)}) %collective-permute-start.2) | collective-permute-done | bytes 524320 | tf_op jit(solution)/shard_map/ppermute | solution.py:282
  47.9 8.8 %far.2 = bf16[8,2,256,128]{3,2,1,0:T(8,128)(2,1)} custom-call(bf16[2,2048,256]{2,1,0:T(8,128)(2,1)} %get-tuple-element.24.q_ref, bf16[8,2,2,64,128]{4,3,2,1,0:T(8,128)(2,1)} %collective-permute-done.refs_0_.refs_2_, bf16[8,2,2,64,128]{4,3,2,1,0:T(8,128)(2,1)} %collective-permute-done.2.refs_1_.refs_3_, ...), custom_call_target="tpu_custom_call" | custom-call | flops 67108864 | bytes 16384 | tf_op jit(solution)/shard_map/far/pallas_call | solution.py:224
  56.8 0.0 all-to-all-done.2.refs_0_.refs_2_
  56.8 0.2 collective-permute-start.4
  57.0 1.3 %collective-permute-start.3 = (bf16[8,2,2,64,128]{4,3,2,1,0:T(8,128)(2,1)}, bf16[8,2,2,64,128]{4,3,2,1,0:T(8,128)(2,1)}, u32[]{:S(2)}, u32[]{:S(2)}) collective-permute-start(bf16[8,2,2,64,128]{4,3,2,1,0:T(8,128)(2,1)} %all-to-all-done.2.refs_0_.refs_2_), channel_id=1, source_target_pairs={{0,128},{1,129},{2,130},{3,131},{4,132},{5,133},{6,134},{7,135},{8... | collective-permute-start | bytes 1572872 | tf_op jit(solution)/shard_map/ppermute | solution.py:287
  58.3 6.1 %all-to-all-start.1 = ((bf16[8,2,256,128]{3,2,1,0:T(8,128)(2,1)}), bf16[8,2,256,128]{3,2,1,0:T(8,128)(2,1)}, u32[]{:S(2)}, u32[]{:S(2)}) async-start(bf16[8,2,256,128]{3,2,1,0:T(8,128)(2,1)} %far.2), calls=%async_computation.1 | async-start | bytes 2097152 | tf_op jit(solution)/shard_map/all_to_all | solution.py:271
  64.3 0.0 collective-permute-done.4.refs_1_.refs_3_
  64.3 8.1 %own.3 = (f32[2,2048,128]{2,1,0:T(8,128)}, f32[2,2048,128]{2,1,0:T(8,128)}) custom-call(bf16[2,2048,256]{2,1,0:T(8,128)(2,1)} %get-tuple-element.32.q_ref, bf16[8,2,2,64,128]{4,3,2,1,0:T(8,128)(2,1)} %all-to-all-done.2.refs_0_.refs_2_, bf16[8,2,2,64,128]{4,3,2,1,0:T(8,128)(2,1)} %collective-permute-done.4.refs_1_.refs_3_, ...), custom_call_target="tpu_custom_call" | custom-call | flops 67108864 | bytes 16384 | tf_op jit(solution)/shard_map/own/pallas_call | solution.py:224
  72.4 1.5 %collective-permute-done.3.refs_0_.refs_2_ = bf16[8,2,2,64,128]{4,3,2,1,0:T(8,128)(2,1)} collective-permute-done((bf16[8,2,2,64,128]{4,3,2,1,0:T(8,128)(2,1)}, bf16[8,2,2,64,128]{4,3,2,1,0:T(8,128)(2,1)}, u32[]{:S(2)}, u32[]{:S(2)}) %collective-permute-start.3) | collective-permute-done | bytes 524320 | tf_op jit(solution)/shard_map/ppermute | solution.py:287
  73.9 0.0 collective-permute-start.5
  74.0 2.2 %collective-permute-done.5.refs_1_.refs_3_ = bf16[8,2,2,64,128]{4,3,2,1,0:T(8,128)(2,1)} collective-permute-done((bf16[8,2,2,64,128]{4,3,2,1,0:T(8,128)(2,1)}, bf16[8,2,2,64,128]{4,3,2,1,0:T(8,128)(2,1)}, u32[]{:S(2)}, u32[]{:S(2)}) %collective-permute-start.5) | collective-permute-done | bytes 524320 | tf_op jit(solution)/shard_map/ppermute | solution.py:290
  76.2 8.8 %far.3 = bf16[8,2,256,128]{3,2,1,0:T(8,128)(2,1)} custom-call(bf16[2,2048,256]{2,1,0:T(8,128)(2,1)} %get-tuple-element.32.q_ref, bf16[8,2,2,64,128]{4,3,2,1,0:T(8,128)(2,1)} %collective-permute-done.3.refs_0_.refs_2_, bf16[8,2,2,64,128]{4,3,2,1,0:T(8,128)(2,1)} %collective-permute-done.5.refs_1_.refs_3_, ...), custom_call_target="tpu_custom_call" | custom-call | flops 67108864 | bytes 16384 | tf_op jit(solution)/shard_map/far/pallas_call | solution.py:224
  85.0 0.0 all-to-all-done.1.x0_ref
  85.0 23.6 %all_to_all.20.x1_ref = bf16[8,2,256,128]{3,2,1,0:T(8,128)(2,1)} all-to-all(bf16[8,2,256,128]{3,2,1,0:T(8,128)(2,1)} %far.3), channel_id=1, replica_groups=mesh['x_lo'=2,'z'=8,'core'=2,'x_hi'=2,'y'=4] {'x_hi','y'}, dimensions={0} | all-to-all | bytes 2097152 | tf_op jit(solution)/shard_map/all_to_all | solution.py:271
  108.6 4.0 %assemble.1 = bf16[256,32,128]{2,1,0:T(8,128)(2,1)} custom-call(bf16[8,2,256,128]{3,2,1,0:T(8,128)(2,1)} %all-to-all-done.1.x0_ref, bf16[8,2,256,128]{3,2,1,0:T(8,128)(2,1)} %all_to_all.20.x1_ref), custom_call_target="tpu_custom_call" | custom-call | tf_op jit(solution)/shard_map/assemble/pallas_call | solution.py:251
Async XLA Ops:
  3.1 26.1 %all-to-all-start = ((bf16[8,2,2,64,128]{4,3,2,1,0:T(8,128)(2,1)}), bf16[8,2,2,64,128]{4,3,2,1,0:T(8,128)(2,1)}, u32[]{:S(2)}, u32[]{:S(2)}) async-start(bf16[8,2,2,64,128]{4,3,2,1,0:T(8,128)(2,1)} %get-tuple-element.25), calls=%async_computation | async-start | bytes 1048576 | tf_op jit(solution)/shard_map/all_to_all | solution.py:270
  29.1 5.5 %collective-permute-start.1 = (bf16[8,2,2,64,128]{4,3,2,1,0:T(8,128)(2,1)}, bf16[8,2,2,64,128]{4,3,2,1,0:T(8,128)(2,1)}, u32[]{:S(2)}, u32[]{:S(2)}) collective-permute-start(bf16[8,2,2,64,128]{4,3,2,1,0:T(8,128)(2,1)} %all-to-all-done.refs_0_.refs_2_), channel_id=1, source_target_pairs={{0,8},{8,0},{1,9},{9,1},{2,10},{10,2},{3,11},{11,3},{4,12},{12,4},... | collective-permute-start | bytes 1572872 | tf_op jit(solution)/shard_map/ppermute | solution.py:278
  29.2 16.5 %collective-permute-start = (bf16[8,2,2,64,128]{4,3,2,1,0:T(8,128)(2,1)}, bf16[8,2,2,64,128]{4,3,2,1,0:T(8,128)(2,1)}, u32[]{:S(2)}, u32[]{:S(2)}) collective-permute-start(bf16[8,2,2,64,128]{4,3,2,1,0:T(8,128)(2,1)} %all-to-all-done.refs_0_.refs_2_), channel_id=1, source_target_pairs={{0,128},{1,129},{2,130},{3,131},{4,132},{5,133},{6,134},{7,135},{8... | collective-permute-start | bytes 1572872 | tf_op jit(solution)/shard_map/ppermute | solution.py:279
  30.5 26.3 %all-to-all-start.2 = ((bf16[8,2,2,64,128]{4,3,2,1,0:T(8,128)(2,1)}), bf16[8,2,2,64,128]{4,3,2,1,0:T(8,128)(2,1)}, u32[]{:S(2)}, u32[]{:S(2)}) async-start(bf16[8,2,2,64,128]{4,3,2,1,0:T(8,128)(2,1)} %get-tuple-element.34), calls=%async_computation.2 | async-start | bytes 1048576 | tf_op jit(solution)/shard_map/all_to_all | solution.py:270
  45.7 2.3 %collective-permute-start.2 = (bf16[8,2,2,64,128]{4,3,2,1,0:T(8,128)(2,1)}, bf16[8,2,2,64,128]{4,3,2,1,0:T(8,128)(2,1)}, u32[]{:S(2)}, u32[]{:S(2)}) collective-permute-start(bf16[8,2,2,64,128]{4,3,2,1,0:T(8,128)(2,1)} %collective-permute-done.refs_0_.refs_2_), channel_id=1, source_target_pairs={{0,8},{8,0},{1,9},{9,1},{2,10},{10,2},{3,11},{11,3},{4,12},{12,4},... | collective-permute-start | bytes 1572872 | tf_op jit(solution)/shard_map/ppermute | solution.py:282
  56.8 7.6 %collective-permute-start.4 = (bf16[8,2,2,64,128]{4,3,2,1,0:T(8,128)(2,1)}, bf16[8,2,2,64,128]{4,3,2,1,0:T(8,128)(2,1)}, u32[]{:S(2)}, u32[]{:S(2)}) collective-permute-start(bf16[8,2,2,64,128]{4,3,2,1,0:T(8,128)(2,1)} %all-to-all-done.2.refs_0_.refs_2_), channel_id=1, source_target_pairs={{0,8},{8,0},{1,9},{9,1},{2,10},{10,2},{3,11},{11,3},{4,12},{12,4},... | collective-permute-start | bytes 1572872 | tf_op jit(solution)/shard_map/ppermute | solution.py:286
  57.0 17.0 %collective-permute-start.3 = (bf16[8,2,2,64,128]{4,3,2,1,0:T(8,128)(2,1)}, bf16[8,2,2,64,128]{4,3,2,1,0:T(8,128)(2,1)}, u32[]{:S(2)}, u32[]{:S(2)}) collective-permute-start(bf16[8,2,2,64,128]{4,3,2,1,0:T(8,128)(2,1)} %all-to-all-done.2.refs_0_.refs_2_), channel_id=1, source_target_pairs={{0,128},{1,129},{2,130},{3,131},{4,132},{5,133},{6,134},{7,135},{8... | collective-permute-start | bytes 1572872 | tf_op jit(solution)/shard_map/ppermute | solution.py:287
  58.3 26.7 %all-to-all-start.1 = ((bf16[8,2,256,128]{3,2,1,0:T(8,128)(2,1)}), bf16[8,2,256,128]{3,2,1,0:T(8,128)(2,1)}, u32[]{:S(2)}, u32[]{:S(2)}) async-start(bf16[8,2,256,128]{3,2,1,0:T(8,128)(2,1)} %far.2), calls=%async_computation.1 | async-start | bytes 2097152 | tf_op jit(solution)/shard_map/all_to_all | solution.py:271
  73.9 2.3 %collective-permute-start.5 = (bf16[8,2,2,64,128]{4,3,2,1,0:T(8,128)(2,1)}, bf16[8,2,2,64,128]{4,3,2,1,0:T(8,128)(2,1)}, u32[]{:S(2)}, u32[]{:S(2)}) collective-permute-start(bf16[8,2,2,64,128]{4,3,2,1,0:T(8,128)(2,1)} %collective-permute-done.3.refs_0_.refs_2_), channel_id=1, source_target_pairs={{0,8},{8,0},{1,9},{9,1},{2,10},{10,2},{3,11},{11,3},{4,12},{12,4},... | collective-permute-start | bytes 1572872 | tf_op jit(solution)/shard_map/ppermute | solution.py:290
